TPU v7x, 512 devices: a whole 4x8x8 slice. The times are simulated.
512 devices in a mesh: dp: 16 (over y, core), group: 32 (over x, z).
Axes of the slice: x: 4, y: 8, z: 8, core: 2. Of those that a mesh axis runs over, the one named last changes fastest.
Arguments:
- queries: bfloat16 [65536, 4096], P(('dp', 'group')), may hold values from -6 to 6
- out_grad: bfloat16 [65536, 4096], P(('dp', 'group')), may hold values from -6 to 6
- encodings: bfloat16 [512, 128, 448], P(('dp', 'group')), may hold values from -6 to 6
- key_weight: bfloat16 [448, 4096], P(None, 'group'), may hold values from -0.25 to 0.25
- value_weight: bfloat16 [448, 4096], P(None, 'group'), may hold values from -0.25 to 0.25
- nbr_ids: int32 [1024, 2], P(('dp', 'group')), may hold values from 0 to 511, as said below
Outputs:
- query_grad: bfloat16 [65536, 4096], P(('dp', 'group'))
- enc_grad: bfloat16 [512, 128, 448], P(('dp', 'group'))
- key_weight_grad: float32 [448, 4096], P(None, 'group')
- value_weight_grad: float32 [448, 4096], P(None, 'group')
Inputs may be any that keep to these rules, and one draw needn't show every extreme that they name: Each span names two different neighbours, both in its own data group's database: nbr_ids[c, j] // 32 equals c // 64.
All inputs are finite; a program needn't handle non-finite values.
Results may differ from a plain program's by a relative error of at most 0.025.
Values may be sent and summed in bfloat16 or wider, within the bound.
A program may use at most 128 MiB of HBM per device.

v0:
```python
import jax
import jax.numpy as jnp
from jax import lax
from jax.sharding import PartitionSpec as P

HEAD_DIM = 128
SPAN = 64
NLEN = 128


def attend(query_block, grad_block, key_rows, value_rows, slot_ids):
    span_count, span_len, block_width = query_block.shape
    head_count = block_width // HEAD_DIM
    scale = HEAD_DIM ** (-0.5)
    flat_ids = slot_ids.reshape(-1)
    key_chosen = jnp.take(key_rows, flat_ids, axis=0).reshape(
        span_count, 2 * NLEN, head_count, HEAD_DIM
    )
    value_chosen = jnp.take(value_rows, flat_ids, axis=0).reshape(
        span_count, 2 * NLEN, head_count, HEAD_DIM
    )
    query_four = query_block.reshape(span_count, span_len, head_count, HEAD_DIM)
    grad_four = grad_block.reshape(span_count, span_len, head_count, HEAD_DIM)
    scores = (
        jnp.einsum("cqhd,ckhd->chqk", query_four, key_chosen, preferred_element_type=jnp.float32)
        * scale
    )
    expo = jnp.exp(scores)
    weights = expo / jnp.sum(expo, axis=-1, keepdims=True)
    weights_bf = weights.astype(jnp.bfloat16)
    weight_grad = jnp.einsum(
        "cqhd,ckhd->chqk", grad_four, value_chosen, preferred_element_type=jnp.float32
    )
    row_delta = jnp.sum(weights * weight_grad, axis=-1, keepdims=True)
    score_grads = (weights * (weight_grad - row_delta) * scale).astype(jnp.bfloat16)
    query_grads = jnp.einsum(
        "chqk,ckhd->cqhd", score_grads, key_chosen, preferred_element_type=jnp.float32
    ).astype(jnp.bfloat16)
    key_slots = jnp.einsum(
        "chqk,cqhd->ckhd", score_grads, query_four, preferred_element_type=jnp.float32
    )
    value_slots = jnp.einsum(
        "chqk,cqhd->ckhd", weights_bf, grad_four, preferred_element_type=jnp.float32
    )
    return (
        query_grads.reshape(span_count * span_len, block_width),
        key_slots.reshape(span_count * 2, NLEN, block_width),
        value_slots.reshape(span_count * 2, NLEN, block_width),
    )


def local(queries, out_grad, encodings, key_weight, value_weight, nbr_ids):
    enc_all = lax.all_gather(encodings, "group", axis=0, tiled=True)
    key_rows = jnp.einsum(
        "nte,ef->ntf", enc_all, key_weight, preferred_element_type=jnp.float32
    ).astype(jnp.bfloat16)
    value_rows = jnp.einsum(
        "nte,ef->ntf", enc_all, value_weight, preferred_element_type=jnp.float32
    ).astype(jnp.bfloat16)
    query_heads, grad_heads = (
        lax.all_to_all(queries, "group", split_axis=1, concat_axis=0, tiled=True),
        lax.all_to_all(out_grad, "group", split_axis=1, concat_axis=0, tiled=True),
    )
    group_neigh = enc_all.shape[0]
    id_offset = lax.axis_index("dp") * group_neigh
    slot_ids = lax.all_gather(nbr_ids, "group", axis=0, tiled=True) - id_offset
    span_count = slot_ids.shape[0]
    block_width = query_heads.shape[1]
    query_block = query_heads.reshape(span_count, SPAN, block_width)
    grad_block = grad_heads.reshape(span_count, SPAN, block_width)
    query_grads, key_slots, value_slots = attend(
        query_block, grad_block, key_rows, value_rows, slot_ids
    )
    query_grad = lax.all_to_all(query_grads, "group", split_axis=0, concat_axis=1, tiled=True)
    flat_ids = slot_ids.reshape(-1)
    key_grads = jax.ops.segment_sum(key_slots, flat_ids, num_segments=group_neigh).astype(
        jnp.bfloat16
    )
    value_grads = jax.ops.segment_sum(value_slots, flat_ids, num_segments=group_neigh).astype(
        jnp.bfloat16
    )
    term = jnp.einsum("ntf,ef->nte", key_grads, key_weight, preferred_element_type=jnp.float32)
    enc_grad = lax.psum_scatter(
        (
            term
            + jnp.einsum(
                "ntf,ef->nte", value_grads, value_weight, preferred_element_type=jnp.float32
            )
        ).astype(jnp.bfloat16),
        "group",
        scatter_dimension=0,
        tiled=True,
    )
    key_wgrad = jnp.einsum("nte,ntf->ef", enc_all, key_grads, preferred_element_type=jnp.float32)
    value_wgrad = jnp.einsum(
        "nte,ntf->ef", enc_all, value_grads, preferred_element_type=jnp.float32
    )
    key_weight_grad, value_weight_grad = (
        lax.psum(key_wgrad.astype(jnp.bfloat16), "dp").astype(jnp.float32),
        lax.psum(value_wgrad.astype(jnp.bfloat16), "dp").astype(jnp.float32),
    )
    return (query_grad, enc_grad, key_weight_grad, value_weight_grad)


def solution(mesh):
    in_specs = (
        P(("dp", "group"), None),
        P(("dp", "group"), None),
        P(("dp", "group"), None, None),
        P(None, "group"),
        P(None, "group"),
        P(("dp", "group"), None),
    )
    out_specs = (
        P(("dp", "group"), None),
        P(("dp", "group"), None, None),
        P(None, "group"),
        P(None, "group"),
    )
    return jax.shard_map(local, mesh=mesh, in_specs=in_specs, out_specs=out_specs, check_vma=False)
```

profile of v0, /device:TPU:1, one launch (start us, length us, event | category | flops | bytes accessed | tf_op | source)
XLA Modules:
  0.0 572.8 jit_solution(6485285691125748825)
XLA Ops:
  9.7 13.7 %all-to-all-start.1 = ((bf16[128,32,128]{2,0,1:T(8,128)(2,1)}), bf16[128,32,128]{2,0,1:T(8,128)(2,1)S(1)}, u32[]{:S(2)}, u32[]{:S(2)}) async-start(bf16[128,32,128]{2,0,1:T(8,128)(2,1)} %copy_bitcast_fusion.1), calls=%async_computation.1 | async-start | bytes 2097152 | tf_op jit(solution)/shard_map/all_to_all | solution.py:62
  23.4 55.3 %all-gather = s32[32,2,2]{2,1,0:T(2,128)S(1)} all-gather(s32[1,2,2]{2,1,0:T(2,128)S(1)} %bitcast.140), channel_id=1, replica_groups=mesh['dp'=16,'group'=32] {'group'}, dimensions={0}, use_global_device_ids=true | all-gather | bytes 528 | tf_op jit(solution)/shard_map/all_gather | solution.py:66
  80.1 7.2 %all-to-all-start = ((bf16[128,32,128]{2,0,1:T(8,128)(2,1)}), bf16[128,32,128]{2,0,1:T(8,128)(2,1)S(1)}, u32[]{:S(2)}, u32[]{:S(2)}) async-start(bf16[128,32,128]{2,0,1:T(8,128)(2,1)} %copy_bitcast_fusion.2), calls=%async_computation | async-start | bytes 2097152 | tf_op jit(solution)/shard_map/all_to_all | solution.py:61
  87.4 30.6 %all-gather.3.cloned.1.call-done = bf16[32,128,448]{1,2,0:T(8,128)(2,1)} async-done(((bf16[1,128,448]{1,2,0:T(8,128)(2,1)}), bf16[32,128,448]{1,2,0:T(8,128)(2,1)}) %all-gather.3.cloned.1.call-update) | async-done | bytes 3670032 | tf_op jit(solution)/shard_map/all_gather | solution.py:53
  118.0 3.4 convolution_convert_fusion.1
  121.4 3.0 gather_fusion
  124.4 3.4 convolution_convert_fusion
  127.8 3.0 gather_fusion.1
  130.8 5.3 broadcast_select_fusion
  136.2 3.5 fusion.27
  139.7 3.9 bitcast_reduce_fusion
  143.6 2.0 copy-done.4
  145.5 4.5 fusion.4
  150.0 31.7 %fusion.7 = f32[64,256,128]{2,1,0:T(8,128)} fusion(bf16[64,64,128]{2,1,0:T(8,128)(2,1)S(1)} %bitcast.137, f32[64,256,64]{1,2,0:T(8,128)} %fusion.27, f32[64,256,64]{1,2,0:T(8,128)} %copy-done.4, f32[64,64]{1,0:T(8,128)S(1)} %get-tuple-element.9), kind=kOutput, calls=%fused_computation.19 | convolution fusion | flops 277876992 | bytes 17842176 | tf_op jit(solution)/shard_map/chqk,cqhd->ckhd/dot_general | solution.py:39
  181.9 17.0 %scatter_fusion = f32[32,128,128]{2,1,0:T(8,128)S(1)} fusion(f32[32,128,128]{2,1,0:T(8,128)S(1)} %broadcast.23.clone, s32[128]{0:T(128)S(1)} %reshape.90, f32[128,128,128]{2,1,0:T(8,128)} %bitcast.133), kind=kCustom, calls=%fused_computation.2 | custom fusion | flops 2097152 | bytes 25166336 | tf_op jit(solution)/shard_map/scatter-add | solution.py:76
  199.0 4.1 fusion.17
  203.4 17.0 %scatter_fusion.1 = f32[32,128,128]{2,1,0:T(8,128)S(1)} fusion(f32[32,128,128]{2,1,0:T(8,128)S(1)} %broadcast.23.clone.1, s32[128]{0:T(128)S(1)} %reshape.90, f32[128,128,128]{2,1,0:T(8,128)} %bitcast.132), kind=kCustom, calls=%fused_computation.3 | custom fusion | flops 2097152 | bytes 25166336 | tf_op jit(solution)/shard_map/scatter-add | solution.py:79
  220.4 4.6 fusion.13
  225.0 1.8 fusion.12
  227.1 6.0 %add_convert_fusion = bf16[32,128,448]{1,2,0:T(8,128)(2,1)} fusion(f32[32,128,448]{1,2,0:T(8,128)} %fusion.17, f32[32,128,128]{2,1,0:T(8,128)S(1)} %scatter_fusion.1, bf16[448,128]{1,0:T(8,128)(2,1)S(1)} %copy-done.7), kind=kOutput, calls=%fused_computation.5 | convolution fusion | flops 473956352 | bytes 13221888 | tf_op jit(solution)/shard_map/ntf,ef->nte/dot_general | solution.py:86
  233.1 28.8 %fusion.9 = bf16[64,128,64]{1,2,0:T(8,128)(2,1)} fusion(bf16[64,256,128]{2,1,0:T(8,128)(2,1)} %bitcast.130, f32[64,256,64]{1,2,0:T(8,128)} %fusion.27, f32[64,256,64]{1,2,0:T(8,128)} %copy-done.4, f32[64,64]{1,0:T(8,128)S(1)} %get-tuple-element.9), kind=kOutput, calls=%fused_computation.21 | convolution fusion | flops 278401280 | bytes 13647872 | tf_op jit(solution)/shard_map/chqk,ckhd->cqhd/dot_general | solution.py:36
  262.0 7.7 %all-to-all-start.2 = ((bf16[32,128,128]{2,1,0:T(8,128)(2,1)}), bf16[32,128,128]{2,1,0:T(8,128)(2,1)S(1)}, u32[]{:S(2)}, u32[]{:S(2)}) async-start(bf16[32,128,128]{2,1,0:T(8,128)(2,1)} %bitcast.13), calls=%async_computation.2 | async-start | bytes 2097152 | tf_op jit(solution)/shard_map/all_to_all | solution.py:74
  269.6 70.1 %all-reduce.3.cloned.1.call-done = (bf16[448,128]{1,0:T(8,128)(2,1)}, bf16[448,128]{1,0:T(8,128)(2,1)}) async-done(((bf16[448,128]{1,0:T(8,128)(2,1)}, bf16[448,128]{1,0:T(8,128)(2,1)}), (bf16[448,128]{1,0:T(8,128)(2,1)}, bf16[448,128]{1,0:T(8,128)(2,1)})) %all-reduce.3.cloned.1.call-update) | async-done | bytes 229392 | tf_op jit(solution)/shard_map/psum | solution.py:99
  344.0 222.2 %reduce-scatter.2.cloned.1.call-done = bf16[1,128,448]{1,2,0:T(8,128)(2,1)} async-done(((bf16[32,128,448]{1,2,0:T(8,128)(2,1)}), bf16[1,128,448]{1,2,0:T(8,128)(2,1)}) %reduce-scatter.2.cloned.1.call-update) | async-done | bytes 114704 | tf_op jit(solution)/shard_map/reduce_scatter | solution.py:83
  (38 shorter events, 9.0 us)
Async XLA Ops:
  7.2 1.2 copy-start
  7.2 16.2 %copy-start.8 = (s32[2,2]{1,0:T(2,128)S(1)}, s32[2,2]{1,0:T(2,128)}, u32[]{:S(2)}) copy-start(s32[2,2]{1,0:T(2,128)} %param.13) | copy-start | bytes 52
  7.2 71.6 %copy-start.5 = (bf16[128,4096]{1,0:T(8,128)(2,1)S(1)}, bf16[128,4096]{1,0:T(8,128)(2,1)}, u32[]{:S(2)}) copy-start(bf16[128,4096]{1,0:T(8,128)(2,1)} %param.8) | copy-start | bytes 3145732
  7.2 110.8 %all-gather.3.cloned.1.call-start = ((), (), s32[]{:S(2)}) async-start(), calls=%async_computation.4 | async-start | bytes 3784704 | tf_op jit(solution)/shard_map/all_gather | solution.py:53
  8.4 109.6 %copy-start.6 = (bf16[448,128]{1,0:T(8,128)(2,1)S(1)}, bf16[448,128]{1,0:T(8,128)(2,1)}, u32[]{:S(2)}) copy-start(bf16[448,128]{1,0:T(8,128)(2,1)} %param.11) | copy-start | bytes 344068
  9.7 70.5 %all-to-all-start.1 = ((bf16[128,32,128]{2,0,1:T(8,128)(2,1)}), bf16[128,32,128]{2,0,1:T(8,128)(2,1)S(1)}, u32[]{:S(2)}, u32[]{:S(2)}) async-start(bf16[128,32,128]{2,0,1:T(8,128)(2,1)} %copy_bitcast_fusion.1), calls=%async_computation.1 | async-start | bytes 2097152 | tf_op jit(solution)/shard_map/all_to_all | solution.py:62
  80.1 59.6 %all-to-all-start = ((bf16[128,32,128]{2,0,1:T(8,128)(2,1)}), bf16[128,32,128]{2,0,1:T(8,128)(2,1)S(1)}, u32[]{:S(2)}, u32[]{:S(2)}) async-start(bf16[128,32,128]{2,0,1:T(8,128)(2,1)} %copy_bitcast_fusion.2), calls=%async_computation | async-start | bytes 2097152 | tf_op jit(solution)/shard_map/all_to_all | solution.py:61
  87.3 252.3 %all-reduce.3.cloned.1.call-start = ((), (), s32[]{:S(2)}) async-start(), calls=%async_computation.6 | async-start | bytes 458752 | tf_op jit(solution)/shard_map/psum | solution.py:99
  121.4 3.0 copy-start.7
  143.6 2.0 copy-start.4
  199.0 4.1 copy-start.2
  220.4 4.6 copy-start.3
  226.8 339.4 %reduce-scatter.2.cloned.1.call-start = ((), (), s32[]{:S(2)}) async-start(), calls=%async_computation.5 | async-start | bytes 3784704 | tf_op jit(solution)/shard_map/reduce_scatter | solution.py:83
  233.1 333.1 %copy-start.1 = (bf16[128,4096]{1,0:T(8,128)(2,1)S(1)}, bf16[128,4096]{1,0:T(8,128)(2,1)}, u32[]{:S(2)}) copy-start(bf16[128,4096]{1,0:T(8,128)(2,1)} %param.9) | copy-start | bytes 3145732
  262.0 80.9 %all-to-all-start.2 = ((bf16[32,128,128]{2,1,0:T(8,128)(2,1)}), bf16[32,128,128]{2,1,0:T(8,128)(2,1)S(1)}, u32[]{:S(2)}, u32[]{:S(2)}) async-start(bf16[32,128,128]{2,1,0:T(8,128)(2,1)} %bitcast.13), calls=%async_computation.2 | async-start | bytes 2097152 | tf_op jit(solution)/shard_map/all_to_all | solution.py:74
Sparse Core Ops, SparseCore 0:
  11.2 106.7 all-gather.2
  227.0 112.6 all-reduce.2
  345.4 220.8 reduce-scatter.1
where the time goes:
time: 578 us; the launch traced here: 573 us
  waiting for transfers between devices  324 us (56%)
  matrix products  95.6 us (17%)
  blocking collectives  55.3 us (10%)
  other arithmetic  42.7 us (7%)
  starting transfers between devices  28.9 us (5%)
  between operations  13.9 us (2%)
  local copies, waits for them, and re-layouts  12.8 us (2%)
    reduce_scatter x1, waiting for transfers between devices, local(): lax.psum_scatter((term + jnp.einsum('ntf,ef->nte', value_grads, value_wei...  222 us
    psum x1, waiting for transfers between devices, local(): lax.psum(key_wgrad.astype(jnp.bfloat16), 'dp').astype(jnp.float32)  70.1 us
    all_gather x1, blocking collectives, local(): slot_ids = lax.all_gather(nbr_ids, 'group', axis=0, tiled=True) - id_offset  55.3 us
    dot_general x1, matrix products, attend(): jnp.einsum('chqk,cqhd->ckhd', score_grads, query_four, preferred_element_...  31.7 us
    all_gather x1, waiting for transfers between devices, local(): enc_all = lax.all_gather(encodings, 'group', axis=0, tiled=True)  30.6 us
    dot_general x1, matrix products, attend(): jnp.einsum('chqk,ckhd->cqhd', score_grads, key_chosen, preferred_element_...  28.8 us
    scatter-add x1, other arithmetic, local(): jax.ops.segment_sum(key_slots, flat_ids, num_segments=group_neigh)  17 us
    scatter-add x1, other arithmetic, local(): jax.ops.segment_sum(value_slots, flat_ids, num_segments=group_neigh)  17 us
  transfers between devices with their start and end apart: 6, of which 3 were waited for; matrix products, arithmetic and copies ran while one was open for 11% of the time, Pallas kernels for 0%

commit v1 on v0

v1 whole, which is shorter than its diff:
```python
import functools

import jax
import jax.numpy as jnp
from jax import lax
from jax.experimental import pallas as pl
from jax.experimental.pallas import tpu as pltpu
from jax.sharding import PartitionSpec as P

HEAD_DIM = 128
SPAN = 64
NLEN = 128
ENC = 448
NX, NZ, NY = 4, 8, 8
HEADS_DEV = 8
WIDTH = HEADS_DEV * HEAD_DIM
SLOTS = 16
TOK = 128
HALF = ENC // 2
MESH = pl.DeviceIdType.MESH
BF16, F32 = jnp.bfloat16, jnp.float32
VMEM_LIMIT = 60 * 1024 * 1024


class Place:
    def __init__(self):
        self.dp, self.group = lax.axis_index("dp"), lax.axis_index("group")
        self.x, self.z = self.group // NZ, self.group % NZ
        self.y, self.core = self.dp // 2, self.dp % 2

    def at_x(self, step):
        return (self.dp, (self.x + step) % NX * NZ + self.z)

    def at_z(self, step):
        return (self.dp, self.x * NZ + (self.z + step) % NZ)

    def at_y(self, step):
        return ((self.y + step) % NY * 2 + self.core, self.group)

    def sibling(self):
        return (self.y * 2 + 1 - self.core, self.group)


def meet(peers):
    barrier = pltpu.get_barrier_semaphore()
    for peer in peers:
        pl.semaphore_signal(barrier, inc=1, device_id=peer, device_id_type=MESH)
    pl.semaphore_wait(barrier, len(peers))


class Copies:
    def __init__(self, send_sems, recv_sems, local_sems):
        self.send_sems, self.recv_sems, self.local_sems = send_sems, recv_sems, local_sems
        self.remote, self.local = [], []

    def push(self, src, dst, peer):
        at = len(self.remote)
        copy = pltpu.make_async_remote_copy(
            src_ref=src,
            dst_ref=dst,
            send_sem=self.send_sems.at[at],
            recv_sem=self.recv_sems.at[at],
            device_id=peer,
            device_id_type=MESH,
        )
        copy.start()
        self.remote.append(copy)
        return copy

    def move(self, src, dst):
        copy = pltpu.make_async_copy(src, dst, self.local_sems.at[len(self.local)])
        copy.start()
        self.local.append(copy)
        return copy


def cols(index, width):
    return pl.ds(pl.multiple_of(index * width, width), width)


IN_PUSHES, IN_MOVES = 64, 6


def bring_in_kernel(
    q_ref, g_ref, enc_ref, kw_ref, vw_ref, ids_ref, qx_ref, gx_ref, enc_all, w_all, ids_all, send_sems, recv_sems, local_sems
):
    me = Place()
    x, z, core = me.x, me.z, me.core
    meet([me.at_x(1), me.at_x(2), me.at_x(3), me.at_z(1), me.at_z(NZ - 1), me.sibling()])
    run = Copies(send_sems, recv_sems, local_sems)
    own_w = [run.move(kw_ref, w_all.at[0, :, cols(z, TOK)]), run.move(vw_ref, w_all.at[1, :, cols(z, TOK)])]
    own_enc = run.move(enc_ref, enc_all.at[x, z])
    run.move(ids_ref, ids_all.at[x])
    from_x = {}
    for step in (1, 3, 2):
        from_x[NX - step] = run.push(enc_ref, enc_all.at[x, z], me.at_x(step))
    late = [run.push(ids_ref, ids_all.at[x], me.at_x(step)) for step in (1, 2, 3)]
    for copy in own_w:
        copy.wait()
    chunks = ["w", 0, 1, 3, 2]
    arrived = {}
    for hop in range(4):
        for chunk in chunks:
            for way in (1, -1):
                block = (z - way * hop + NZ) % NZ
                if hop == 0 and chunk != "w" and way == 1:
                    if chunk == 0:
                        own_enc.wait()
                    else:
                        from_x[chunk].wait_recv()
                if hop > 0:
                    before = arrived[way, hop - 1, chunk]
                    before.wait_recv()
                if chunk == "w":
                    if hop > 0:
                        part = w_all.at[core, :, cols(block, TOK)]
                        late.append(run.push(part, part, me.sibling()))
                    if hop < 3:
                        part = w_all.at[core, :, cols(block, TOK)]
                    else:
                        part = w_all.at[core, pl.ds(0 if way == 1 else HALF, HALF), cols(block, TOK)]
                else:
                    if hop == 3 and (chunk in (0, 1)) != (way == 1):
                        continue
                    part = enc_all.at[(x + chunk) % NX, block]
                arrived[way, hop, chunk] = run.push(part, part, me.at_z(way))
        if hop == 0:
            for src, dst in ((q_ref, qx_ref), (g_ref, gx_ref)):
                for step in (1, 3, 2):
                    peer = me.at_x(step)
                    late.append(run.push(src.at[:, cols((x + step) % NX, WIDTH)], dst.at[x], peer))
                run.move(src.at[:, cols(x, WIDTH)], dst.at[x])
    far = (z + 4) % NZ
    for way in (1, -1):
        arrived[way, 3, "w"].wait_recv()
    part = w_all.at[core, :, cols(far, TOK)]
    late.append(run.push(part, part, me.sibling()))
    for way, chunk in ((1, 0), (1, 1), (-1, 3), (-1, 2)):
        arrived[way, 3, chunk].wait_recv()
    for copy in late:
        copy.wait_recv()
    for copy in run.remote:
        copy.wait_send()
    for copy in run.local[3:]:
        copy.wait()


def bring_in(queries, out_grad, enc_t, key_weight, value_weight, ids):
    whole = pl.BlockSpec(memory_space=pl.ANY)
    return pl.pallas_call(
        bring_in_kernel,
        out_shape=[
            jax.ShapeDtypeStruct((NX, TOK, WIDTH), BF16),
            jax.ShapeDtypeStruct((NX, TOK, WIDTH), BF16),
            jax.ShapeDtypeStruct((NX, NZ, ENC, NLEN), BF16),
            jax.ShapeDtypeStruct((2, ENC, WIDTH), BF16),
            jax.ShapeDtypeStruct((NX, 8, 128), jnp.int32),
        ],
        in_specs=[whole] * 6,
        out_specs=[whole] * 5,
        scratch_shapes=[
            pltpu.SemaphoreType.DMA((IN_PUSHES,)),
            pltpu.SemaphoreType.DMA((IN_PUSHES,)),
            pltpu.SemaphoreType.DMA((IN_MOVES,)),
        ],
        compiler_params=pltpu.CompilerParams(collective_id=0, has_side_effects=True),
    )(queries, out_grad, enc_t, key_weight, value_weight, ids)


def dot(a, b, da=1, db=0):
    return lax.dot_general(a, b, (((da,), (db,)), ((), ())), preferred_element_type=F32)


def attend_kernel(ids_ref, q_ref, g_ref, enc_ref, w_ref, qg_ref, part_ref, wg_ref, enc_sel, w_t, kv_t, slots_t, total):
    scale = HEAD_DIM ** (-0.5)

    def id_of(slot):
        return ids_ref[slot // 4, slot // 2 % 2, slot % 2]

    for slot in range(SLOTS):
        enc_sel[:, slot * NLEN : (slot + 1) * NLEN] = enc_ref[id_of(slot)]
    for kind in range(2):
        for head in range(HEADS_DEV):
            at = kind * WIDTH + head * HEAD_DIM
            w_t[at : at + HEAD_DIM, :] = w_ref[kind, :, head * HEAD_DIM : (head + 1) * HEAD_DIM].T
    total[...] = jnp.zeros_like(total)

    @pl.loop(0, 8)
    def _(span):
        here = cols(span, 2 * NLEN)
        chosen = enc_sel[:, here]
        for tile in range(4):
            rows = pl.ds(tile * 512, 512)
            kv_t[rows, here] = dot(w_t[rows, :], chosen).astype(BF16)

    @pl.loop(0, 8)
    def _(span):
        here = cols(span, 2 * NLEN)
        source, rows = span // 2, cols(span % 2, SPAN)
        for head in range(HEADS_DEV):
            lanes = pl.ds(head * HEAD_DIM, HEAD_DIM)
            query, grad = q_ref[source, rows, lanes], g_ref[source, rows, lanes]
            key_t = kv_t[head * HEAD_DIM : (head + 1) * HEAD_DIM, here]
            value_t = kv_t[WIDTH + head * HEAD_DIM : WIDTH + (head + 1) * HEAD_DIM, here]
            scores = dot(query, key_t)
            weight_grad = dot(grad, value_t)
            expo = jnp.exp((scores - jnp.max(scores, axis=-1, keepdims=True)) * scale)
            weights = expo * (1.0 / jnp.sum(expo, axis=-1, keepdims=True))
            row_delta = jnp.sum(weights * weight_grad, axis=-1, keepdims=True)
            score_grads = (weights * (weight_grad - row_delta) * scale).astype(BF16)
            qg_ref[source, rows, lanes] = dot(score_grads, key_t, 1, 1).astype(BF16)
            slots_t[head * HEAD_DIM : (head + 1) * HEAD_DIM, here] = dot(query, score_grads, 0, 0).astype(BF16)
            slots_t[WIDTH + head * HEAD_DIM : WIDTH + (head + 1) * HEAD_DIM, here] = dot(
                grad, weights.astype(BF16), 0, 0
            ).astype(BF16)

    for kind in range(2):

        @pl.loop(0, 4)
        def _(tile):
            rows = pl.ds(pl.multiple_of(kind * WIDTH + tile * 256, 256), 256)
            wg_ref[kind, :, cols(tile, 256)] = dot(enc_sel[...], slots_t[rows, :], 1, 1).astype(BF16)

    @pl.loop(0, 8)
    def _(span):
        here = cols(span, 2 * NLEN)
        both = dot(w_ref[0], slots_t[0:WIDTH, here]) + dot(w_ref[1], slots_t[WIDTH:, here])
        total[id_of(2 * span)] += both[:, 0:NLEN]
        total[id_of(2 * span + 1)] += both[:, NLEN:]

    @pl.loop(0, NX * NZ)
    def _(block):
        part_ref[block] = total[block].astype(BF16)


def attend(ids, queries, grads, enc_all, w_all):
    vmem = pl.BlockSpec(memory_space=pltpu.VMEM)
    return pl.pallas_call(
        attend_kernel,
        out_shape=[
            jax.ShapeDtypeStruct((NX, TOK, WIDTH), BF16),
            jax.ShapeDtypeStruct((NX * NZ, ENC, NLEN), BF16),
            jax.ShapeDtypeStruct((2, ENC, WIDTH), BF16),
        ],
        in_specs=[pl.BlockSpec(memory_space=pltpu.SMEM)] + [vmem] * 4,
        out_specs=[vmem] * 3,
        scratch_shapes=[
            pltpu.VMEM((ENC, SLOTS * NLEN), BF16),
            pltpu.VMEM((2 * WIDTH, ENC), BF16),
            pltpu.VMEM((2 * WIDTH, SLOTS * NLEN), BF16),
            pltpu.VMEM((2 * WIDTH, SLOTS * NLEN), BF16),
            pltpu.VMEM((NX * NZ, ENC, NLEN), F32),
        ],
        compiler_params=pltpu.CompilerParams(vmem_limit_bytes=VMEM_LIMIT),
    )(ids, queries, grads, enc_all, w_all)


OUT_PUSHES, OUT_MOVES = 64, 1


def send_out_kernel(
    qg_ref, part_ref, wg_ref, out_q, out_enc, out_k, out_v,
    landed, pair, w_sum, x_sum, x_landed, y_sum, y_landed, w_own, w_other, send_sems, recv_sems, local_sems
):
    me = Place()
    x, z, core = me.x, me.z, me.core
    meet(
        [me.at_x(1), me.at_x(2), me.at_x(3), me.at_z(1), me.at_z(NZ - 1), me.sibling()]
        + [me.at_y(step) for step in range(1, NY)]
    )
    run = Copies(send_sems, recv_sems, local_sems)
    late = []
    from_sibling = run.push(wg_ref.at[1 - core], pair, me.sibling())
    arrived = {}
    for chunk, way in ((0, 1), (2, -1), (1, 1), (3, -1)):
        arrived[way, 0, chunk] = run.push(part_ref.at[chunk, (z + 4) % NZ], landed.at[(1 - way) // 2, 0, chunk], me.at_z(way))
    for step in (1, 3, 2):
        late.append(run.push(qg_ref.at[(x + step) % NX], out_q.at[:, cols(x, WIDTH)], me.at_x(step)))
    run.move(qg_ref.at[x], out_q.at[:, cols(x, WIDTH)])
    from_sibling.wait_recv()
    for block in range(NZ):
        here = slice(block * TOK, (block + 1) * TOK)
        w_sum[block] = (wg_ref[core, :, here].astype(F32) + pair[:, here].astype(F32)).astype(BF16)
    for way in (1, -1):
        rows = pl.ds(0 if way == 1 else HALF, HALF)
        arrived[way, 0, 4] = run.push(
            w_sum.at[(z + 4) % NZ, rows], landed.at[(1 - way) // 2, 0, 4, rows], me.at_z(way)
        )
    for hop in range(1, 4):
        for chunk in (4, 0, 2, 1, 3):
            for way in (1, -1):
                lane = (1 - way) // 2
                block = (z + way * (4 - hop) + NZ) % NZ
                slot = landed.at[lane, hop - 1, chunk]
                own = w_sum.at[block] if chunk == 4 else part_ref.at[chunk, block]
                source = slot
                if (way, hop - 1, chunk) in arrived:
                    arrived[way, hop - 1, chunk].wait_recv()
                    if hop == 1 and chunk == 4:
                        mine, rest = (0, HALF) if way == 1 else (HALF, 0)
                        mine, rest = slice(mine, mine + HALF), slice(rest, rest + HALF)
                        slot[mine] = (slot[mine].astype(F32) + own[mine].astype(F32)).astype(BF16)
                        slot[rest] = own[rest]
                    else:
                        slot[...] = (slot[...].astype(F32) + own[...].astype(F32)).astype(BF16)
                else:
                    source = own
                arrived[way, hop, chunk] = run.push(source, landed.at[lane, hop, chunk], me.at_z(way))
    for way in (1, -1):
        arrived[way, 3, 4].wait_recv()
    y_sum[...] = (w_sum[z].astype(F32) + landed[0, 3, 4].astype(F32) + landed[1, 3, 4].astype(F32)).astype(BF16)
    from_y = [run.push(y_sum, y_landed.at[step - 1], me.at_y(step)) for step in range(1, NY)]
    from_x = {}
    for chunk in (0, 2, 1, 3):
        for way in (1, -1):
            arrived[way, 3, chunk].wait_recv()
        x_sum[chunk] = (
            part_ref[chunk, z].astype(F32) + landed[0, 3, chunk].astype(F32) + landed[1, 3, chunk].astype(F32)
        ).astype(BF16)
    for step in (1, 3, 2):
        from_x[step] = run.push(x_sum.at[(x + step) % NX], x_landed.at[step - 1], me.at_x(step))
    whole = y_sum[...].astype(F32)
    for step in range(1, NY):
        from_y[step - 1].wait_recv()
        whole += y_landed[step - 1].astype(F32)
    w_own[...] = whole
    from_sibling = run.push(w_own, w_other, me.sibling())
    enc = x_sum[x].astype(F32)
    for step in (1, 3, 2):
        from_x[step].wait_recv()
        enc += x_landed[step - 1].astype(F32)
    out_enc[...] = enc.astype(BF16)
    from_sibling.wait_recv()

    @pl.when(core == 0)
    def _():
        out_k[...] = w_own[...]
        out_v[...] = w_other[...]

    @pl.when(core == 1)
    def _():
        out_k[...] = w_other[...]
        out_v[...] = w_own[...]

    for copy in late:
        copy.wait_recv()
    for copy in run.remote:
        copy.wait_send()
    for copy in run.local:
        copy.wait()


def send_out(query_grads, part, weight_grads):
    whole, vmem = pl.BlockSpec(memory_space=pl.ANY), pl.BlockSpec(memory_space=pltpu.VMEM)
    block = (ENC, NLEN)
    return pl.pallas_call(
        send_out_kernel,
        out_shape=[
            jax.ShapeDtypeStruct((TOK, NX * WIDTH), BF16),
            jax.ShapeDtypeStruct(block, BF16),
            jax.ShapeDtypeStruct(block, F32),
            jax.ShapeDtypeStruct(block, F32),
        ],
        in_specs=[whole, vmem, vmem],
        out_specs=[whole, vmem, vmem, vmem],
        scratch_shapes=[
            pltpu.VMEM((2, 4, 5) + block, BF16),
            pltpu.VMEM((ENC, WIDTH), BF16),
            pltpu.VMEM((NZ,) + block, BF16),
            pltpu.VMEM((NX,) + block, BF16),
            pltpu.VMEM((NX - 1,) + block, BF16),
            pltpu.VMEM(block, BF16),
            pltpu.VMEM((NY - 1,) + block, BF16),
            pltpu.VMEM(block, F32),
            pltpu.VMEM(block, F32),
            pltpu.SemaphoreType.DMA((OUT_PUSHES,)),
            pltpu.SemaphoreType.DMA((OUT_PUSHES,)),
            pltpu.SemaphoreType.DMA((OUT_MOVES,)),
        ],
        compiler_params=pltpu.CompilerParams(collective_id=1, has_side_effects=True, vmem_limit_bytes=VMEM_LIMIT),
    )(query_grads, part, weight_grads)


def local(queries, out_grad, encodings, key_weight, value_weight, nbr_ids):
    enc_t = jnp.swapaxes(encodings[0], 0, 1)
    ids = jnp.pad(nbr_ids - lax.axis_index("dp") * (NX * NZ), ((0, 6), (0, 126)))
    q_x, g_x, enc_all, w_all, ids_all = bring_in(queries, out_grad, enc_t, key_weight, value_weight, ids)
    query_grads, part, weight_grads = attend(ids_all, q_x, g_x, enc_all.reshape(NX * NZ, ENC, NLEN), w_all)
    query_grad, enc_grad, key_grad, value_grad = send_out(
        query_grads, part.reshape(NX, NZ, ENC, NLEN), weight_grads
    )
    return query_grad, jnp.swapaxes(enc_grad, 0, 1)[None], key_grad, value_grad


def solution(mesh):
    in_specs = (
        P(("dp", "group"), None),
        P(("dp", "group"), None),
        P(("dp", "group"), None, None),
        P(None, "group"),
        P(None, "group"),
        P(("dp", "group"), None),
    )
    out_specs = (
        P(("dp", "group"), None),
        P(("dp", "group"), None, None),
        P(None, "group"),
        P(None, "group"),
    )
    return jax.shard_map(local, mesh=mesh, in_specs=in_specs, out_specs=out_specs, check_vma=False)
```

time: 578 us -> 198 us (0.34)
  waiting for transfers between devices: 324 us -> 0 us
  Pallas kernels: 0 us -> 189 us
  matrix products: 95.6 us -> 0 us
  blocking collectives: 55.3 us -> 0 us
  other arithmetic: 42.7 us -> 0.68 us
  starting transfers between devices: 28.9 us -> 0 us
  between operations: 13.9 us -> 0.65 us
    reduce_scatter x1 -> x0, waiting for transfers between devices: 222 us -> none  [local(): lax.psum_scatter((term + jnp.einsum('ntf,ef->nte', value_grads, value_wei...]
    pallas_call x0 -> x3, Pallas kernels: none -> 189 us  [the longest x1 69.1 us: send_out(): pl.pallas_call(send_out_kernel, out_shape=[jax.ShapeDtypeStruct((TOK, NX...]
    dot_general x11 -> x0, matrix products: 95.6 us -> none  [the longest x1 31.7 us: attend(): jnp.einsum('chqk,cqhd->ckhd', score_grads, query_four, preferred_element_...]
    psum x1 -> x0, waiting for transfers between devices: 70.1 us -> none  [local(): lax.psum(key_wgrad.astype(jnp.bfloat16), 'dp').astype(jnp.float32)]
    all_gather x1 -> x0, blocking collectives: 55.3 us -> none  [local(): slot_ids = lax.all_gather(nbr_ids, 'group', axis=0, tiled=True) - id_offset]
    scatter-add x2 -> x0, other arithmetic: 34.1 us -> none  [the longest x1 17 us: local(): jax.ops.segment_sum(key_slots, flat_ids, num_segments=group_neigh)]
    all_gather x1 -> x0, waiting for transfers between devices: 30.6 us -> none  [local(): enc_all = lax.all_gather(encodings, 'group', axis=0, tiled=True)]
    all_to_all x3 -> x0, starting transfers between devices: 28.6 us -> none  [the longest x1 13.7 us: local(): lax.all_to_all(out_grad, 'group', split_axis=1, concat_axis=0, tiled=True)]
  transfers between devices with their start and end apart: 6 -> 0, of which waited for: 3 -> 0; matrix products, arithmetic and copies ran while one was open for 11% -> 0% of each run, Pallas kernels for 0% -> 0%
where the time goes in v1:
time: 198 us
  Pallas kernels  189 us (95%)
  local copies, waits for them, and re-layouts  7.72 us (4%)
    pallas_call x1, Pallas kernels, send_out(): pl.pallas_call(send_out_kernel, out_shape=[jax.ShapeDtypeStruct((TOK, NX...  69.1 us
    pallas_call x1, Pallas kernels, bring_in(): pl.pallas_call(bring_in_kernel, out_shape=[jax.ShapeDtypeStruct((NX, TOK,...  66.9 us
    pallas_call x1, Pallas kernels, attend(): pl.pallas_call(attend_kernel, out_shape=[jax.ShapeDtypeStruct((NX, TOK, W...  53 us
    unnamed x4, local copies, waits for them, and re-layouts  7.12 us

profile of v1, /device:TPU:1, one launch (start us, length us, event | category | flops | bytes accessed | tf_op | source)
XLA Modules:
  0.0 198.1 jit_solution(13570539723354964385)
XLA Ops:
  0.6 0.7 broadcast_subtract_fusion
  1.3 0.6 pad.4.ids_ref
  1.9 66.9 %shard_map.93 = (bf16[4,128,1024]{2,1,0:T(8,128)(2,1)}, bf16[4,128,1024]{2,1,0:T(8,128)(2,1)}, bf16[4,8,448,128]{3,2,1,0:T(8,128)(2,1)}, bf16[2,448,1024]{2,1,0:T(8,128)(2,1)}, s32[4,8,128]{2,1,0:T(8,128)}) custom-call(bf16[128,4096]{1,0:T(8,128)(2,1)} %q_ref.1, bf16[128,4096]{1,0:T(8,128)(2,1)} %g_ref.1, bf16[448,128]{1,0:T(8,128)(2,1)} %bitcast.11, ...), custom_call_target="tpu_custom_call" | custom-call | tf_op jit(solution)/shard_map/pallas_call | solution.py:150
  68.8 53.0 %shard_map.94 = (bf16[4,128,1024]{2,1,0:T(8,128)(2,1)}, bf16[32,448,128]{2,1,0:T(8,128)(2,1)}, bf16[2,448,1024]{2,1,0:T(8,128)(2,1)}) custom-call(s32[4,8,128]{2,1,0:T(8,128)} %get-tuple-element.16.ids_ref, bf16[4,128,1024]{2,1,0:T(8,128)(2,1)} %get-tuple-element.17.q_ref, bf16[4,128,1024]{2,1,0:T(8,128)(2,1)} %get-tuple-element.18.g_ref, ...), custom_call_target="tpu_custom_call" | custom-call | tf_op jit(solution)/shard_map/pallas_call | solution.py:238
  121.8 69.1 %shard_map.95 = (bf16[128,4096]{1,0:T(8,128)(2,1)}, bf16[448,128]{1,0:T(8,128)(2,1)}, f32[448,128]{1,0:T(8,128)}, f32[448,128]{1,0:T(8,128)}) custom-call(bf16[4,128,1024]{2,1,0:T(8,128)(2,1)} %get-tuple-element.21.qg_ref, bf16[4,8,448,128]{3,2,1,0:T(8,128)(2,1)} %bitcast.8, bf16[2,448,1024]{2,1,0:T(8,128)(2,1)} %get-tuple-element.23.wg_ref), custom_call_target="tpu_custom_call" | custom-call | tf_op jit(solution)/shard_map/pallas_call | solution.py:356
  191.0 2.3 %copy.14 = bf16[128,4096]{1,0:T(8,128)(2,1)} copy(bf16[128,4096]{1,0:T(8,128)(2,1)} %get-tuple-element.32) | data formatting | bytes 2097152
  193.3 1.6 copy.15
  194.8 1.6 copy.16
  196.4 1.6 copy.17

commit v2 on v0

v2 whole, which is shorter than its diff:
```python
import functools

import jax
import jax.numpy as jnp
from jax import lax
from jax.experimental import pallas as pl
from jax.experimental.pallas import tpu as pltpu
from jax.sharding import PartitionSpec as P

HEAD_DIM = 128
SPAN = 64
NLEN = 128
ENC = 448
NX, NZ, NY = 4, 8, 8
HEADS_DEV = 8
WIDTH = HEADS_DEV * HEAD_DIM
SLOTS = 16
TOK = 128
IN_A = 336
OUT_A = 256
MESH = pl.DeviceIdType.MESH
BF16, F32 = jnp.bfloat16, jnp.float32
VMEM_LIMIT = 60 * 1024 * 1024


class Place:
    def __init__(self):
        self.dp, self.group = lax.axis_index("dp"), lax.axis_index("group")
        self.x, self.z = self.group // NZ, self.group % NZ
        self.y, self.core = self.dp // 2, self.dp % 2

    def at_x(self, step):
        return (self.dp, (self.x + step) % NX * NZ + self.z)

    def at_z(self, step):
        return (self.dp, self.x * NZ + (self.z + step) % NZ)

    def at_y(self, step):
        return ((self.y + step) % NY * 2 + self.core, self.group)

    def sibling(self):
        return (self.y * 2 + 1 - self.core, self.group)


def meet(peers):
    barrier = pltpu.get_barrier_semaphore()
    for peer in peers:
        pl.semaphore_signal(barrier, inc=1, device_id=peer, device_id_type=MESH)
    pl.semaphore_wait(barrier, len(peers))


class Copies:
    def __init__(self, send_sems, recv_sems, local_sems):
        self.send_sems, self.recv_sems, self.local_sems = send_sems, recv_sems, local_sems
        self.remote, self.local = [], []

    def push(self, src, dst, peer):
        at = len(self.remote)
        copy = pltpu.make_async_remote_copy(
            src_ref=src,
            dst_ref=dst,
            send_sem=self.send_sems.at[at],
            recv_sem=self.recv_sems.at[at],
            device_id=peer,
            device_id_type=MESH,
        )
        copy.start()
        self.remote.append(copy)
        return copy

    def move(self, src, dst):
        copy = pltpu.make_async_copy(src, dst, self.local_sems.at[len(self.local)])
        copy.start()
        self.local.append(copy)
        return copy


def cols(index, width):
    return pl.ds(pl.multiple_of(index * width, width), width)


def dot(a, b, da=1, db=0):
    return lax.dot_general(a, b, (((da,), (db,)), ((), ())), preferred_element_type=F32)


class Gather:
    def __init__(self, run, me, view, rows, cut):
        self.run, self.me, self.view, self.arrived = run, me, view, {}
        self.parts = {1: pl.ds(0, cut), -1: pl.ds(cut, rows - cut)}

    def send(self, hop, way, source=None):
        if hop > 0:
            self.arrived[way, hop - 1].wait_recv()
        block = (self.me.z - way * hop + NZ) % NZ
        there = self.view(block)
        here = there if source is None else source
        if hop == 3:
            here, there = here.at[self.parts[way]], there.at[self.parts[way]]
        self.arrived[way, hop] = self.run.push(here, there, self.me.at_z(way))
        return block

    def end(self):
        for way in (1, -1):
            self.arrived[way, 3].wait_recv()


class Reduce:
    def __init__(self, run, me, own, landed, rows, cut):
        self.run, self.me, self.own, self.landed, self.arrived = run, me, own, landed, {}
        self.parts = {1: pl.ds(0, cut), -1: pl.ds(cut, rows - cut)}

    def send(self, hop, way):
        lane = (1 - way) // 2
        own = self.own((self.me.z + way * (4 - hop) + NZ) % NZ)
        part, rest = self.parts[way], self.parts[-way]
        there = self.landed.at[lane, hop]
        if hop == 0:
            source, there = own.at[part], there.at[part]
        else:
            self.arrived[way, hop - 1].wait_recv()
            source = self.landed.at[lane, hop - 1]
            if hop == 1:
                source[part] = (source[part].astype(F32) + own[part].astype(F32)).astype(BF16)
                source[rest] = own[rest]
            else:
                source[...] = (source[...].astype(F32) + own[...].astype(F32)).astype(BF16)
        self.arrived[way, hop] = self.run.push(source, there, self.me.at_z(way))

    def end(self):
        for way in (1, -1):
            self.arrived[way, 3].wait_recv()
        own = self.own(self.me.z)[...].astype(F32)
        return own + self.landed[0, 3].astype(F32) + self.landed[1, 3].astype(F32)


PUSHES, MOVES = 160, 10


def whole_kernel(
    q_ref, g_ref, enc_ref, kw_ref, vw_ref, ids_ref,
    out_q, ids_all, out_enc, out_w,
    q_x, g_x, enc_all, w_all, ids, enc_sel, w_t, kv_t, slots_t, scores, grads, score_bf, weight_bf, qg,
    slot_grads, part, w_part, w_pair, w_sum, land_a, land_b, land_w, x_b, b_sum, a_sum, x_a, y_sum, y_land, y_own, w_own, w_other,
    send_sems, recv_sems, local_sems
):
    me = Place()
    x, z, core = me.x, me.z, me.core
    scale = HEAD_DIM ** (-0.5)
    meet(
        [me.at_x(1), me.at_x(2), me.at_x(3), me.at_z(1), me.at_z(NZ - 1), me.sibling()]
        + [me.at_y(step) for step in range(1, NY)]
    )
    run = Copies(send_sems, recv_sems, local_sems)
    late = []

    in_a, in_b = pl.ds(0, IN_A), pl.ds(IN_A, ENC - IN_A)
    own_w = [run.move(kw_ref, w_all.at[0, :, cols(z, TOK)]), run.move(vw_ref, w_all.at[1, :, cols(z, TOK)])]
    own_enc = run.move(enc_ref, enc_all.at[x, z])
    run.move(ids_ref, ids_all.at[x]).wait()
    gather_b = Gather(run, me, lambda block: enc_all.at[x, block, in_b], ENC - IN_A, 64)
    for way in (1, -1):
        gather_b.send(0, way, enc_ref.at[in_b])
    from_x = {}
    for step in (1, 3, 2):
        from_x[NX - step] = run.push(enc_ref.at[in_a], enc_all.at[x, z, in_a], me.at_x(step))
    lists = [run.push(ids_ref, ids_all.at[x], me.at_x(step)) for step in (1, 2, 3)]
    for copy in own_w:
        copy.wait()
    gather_w = Gather(run, me, lambda block: w_all.at[core, :, cols(block, TOK)], ENC, ENC // 2)
    for way in (1, -1):
        gather_w.send(0, way)
    inputs_x = {step: [] for step in range(NX)}
    for step in (1, 3, 2):
        for src, dst in ((q_ref, q_x), (g_ref, g_x)):
            copy = run.push(src.at[:, cols((x + step) % NX, WIDTH)], dst.at[x], me.at_x(step))
            inputs_x[NX - step].append(copy)
    own_inputs = [run.move(src.at[:, cols(x, WIDTH)], dst.at[x]) for src, dst in ((q_ref, q_x), (g_ref, g_x))]
    gathers_a = {}
    for chunk in (0, 1, 3, 2):
        gathers_a[chunk] = Gather(
            run, me, lambda block, chunk=chunk: enc_all.at[(x + chunk) % NX, block, in_a], IN_A, 176
        )
    own_enc.wait()
    for hop in range(4):
        for way in (1, -1):
            if hop > 0:
                gather_b.send(hop, way)
                block = gather_w.send(hop, way)
                view = gather_w.view(block)
                late.append(run.push(view, view, me.sibling()))
        for chunk in (0, 1, 3, 2):
            if hop == 0 and chunk != 0:
                from_x[chunk].wait_recv()
            for way in (1, -1):
                gathers_a[chunk].send(hop, way)
    gather_b.end()
    blocks_b = enc_all.at[x, :, in_b]
    from_x_b = [run.push(blocks_b, blocks_b, me.at_x(step)) for step in (1, 3, 2)]
    gather_w.end()
    view = gather_w.view((z + 4) % NZ)
    late.append(run.push(view, view, me.sibling()))
    for copy in late:
        copy.wait_recv()
    for kind in range(2):
        for head in range(HEADS_DEV):
            at = kind * WIDTH + head * HEAD_DIM
            w_t[at : at + HEAD_DIM, :] = w_all[kind, :, head * HEAD_DIM : (head + 1) * HEAD_DIM].T
    slot_grads[SLOTS] = jnp.zeros((ENC, NLEN), F32)
    for copy in lists:
        copy.wait_recv()
    run.move(ids_all, ids).wait()
    for chunk in (0, 1, 3, 2):
        gathers_a[chunk].end()
    for copy in from_x_b:
        copy.wait_recv()

    def id_of(slot):
        return ids[slot // 4, slot // 2 % 2, slot % 2]

    for slot in range(SLOTS):
        neighbour = id_of(slot)
        enc_sel[:, slot * NLEN : (slot + 1) * NLEN] = enc_all[neighbour // NZ, neighbour % NZ]

    @pl.loop(0, 8)
    def _(span):
        here = cols(span, 2 * NLEN)
        chosen = enc_sel[:, here]
        for tile in range(4):
            rows = pl.ds(tile * 512, 512)
            kv_t[rows, here] = dot(w_t[rows, :], chosen).astype(BF16)

    for step in (1, 3, 2, 0):
        source = (x + step) % NX
        if step == 0:
            for copy in own_inputs:
                copy.wait()
        else:
            for copy in inputs_x[step]:
                copy.wait_recv()

        @pl.loop(0, 2)
        def _(turn):
            here, rows = cols(source * 2 + turn, 2 * NLEN), cols(turn, SPAN)
            for head in range(HEADS_DEV):
                lanes, tile = pl.ds(head * HEAD_DIM, HEAD_DIM), pl.ds(head * SPAN, SPAN)
                scores[tile, :] = dot(q_x[source, rows, lanes], kv_t[lanes, here])
                grads[tile, :] = dot(g_x[source, rows, lanes], kv_t[pl.ds(WIDTH + head * HEAD_DIM, HEAD_DIM), here])
            expo = scores[...]
            expo = jnp.exp((expo - jnp.max(expo, axis=-1, keepdims=True)) * scale)
            weights = expo * (1.0 / jnp.sum(expo, axis=-1, keepdims=True))
            weight_bf[...] = weights.astype(BF16)
            weight_grad = grads[...]
            row_delta = jnp.sum(weights * weight_grad, axis=-1, keepdims=True)
            score_bf[...] = (weights * (weight_grad - row_delta) * scale).astype(BF16)
            for head in range(HEADS_DEV):
                lanes, tile = pl.ds(head * HEAD_DIM, HEAD_DIM), pl.ds(head * SPAN, SPAN)
                query, grad = q_x[source, rows, lanes], g_x[source, rows, lanes]
                qg[source, rows, lanes] = dot(score_bf[tile, :], kv_t[lanes, here], 1, 1).astype(BF16)
                slots_t[lanes, here] = dot(query, score_bf[tile, :], 0, 0).astype(BF16)
                slots_t[pl.ds(WIDTH + head * HEAD_DIM, HEAD_DIM), here] = dot(grad, weight_bf[tile, :], 0, 0).astype(BF16)

        if step == 0:
            run.move(qg.at[x], out_q.at[x])
        else:
            late.append(run.push(qg.at[source], out_q.at[x], me.at_x(step)))

    def slot_products(rows):
        @pl.loop(0, 8)
        def _(span):
            here = cols(span, 2 * NLEN)
            both = dot(w_all[0, rows, :], slots_t[0:WIDTH, here]) + dot(w_all[1, rows, :], slots_t[WIDTH:, here])
            slot_grads[2 * span, rows] = both[:, 0:NLEN]
            slot_grads[2 * span + 1, rows] = both[:, NLEN:]

    def neighbour_sum(at_x, at_z, rows):
        neighbour = at_x * NZ + at_z
        total = None
        for span in range(8):
            first, second = id_of(2 * span), id_of(2 * span + 1)
            slot = jnp.where(first == neighbour, 2 * span, jnp.where(second == neighbour, 2 * span + 1, SLOTS))
            term = slot_grads[slot, rows]
            total = term if total is None else total + term
        part[at_x, at_z, rows] = total.astype(BF16)

    out_a, out_b = pl.ds(0, OUT_A), pl.ds(OUT_A, ENC - OUT_A)
    slot_products(out_b)
    from_x = []
    for step in (1, 3, 2, 0):
        at_x = (x + step) % NX

        @pl.loop(0, NZ)
        def _(at_z):
            neighbour_sum(at_x, at_z, out_b)

        if step != 0:
            from_x.append(run.push(part.at[at_x, :, out_b], x_b.at[step - 1], me.at_x(step)))
    slot_products(out_a)
    reduces_a = [
        Reduce(run, me, lambda block, chunk=chunk: part.at[chunk, block, out_a], land_a.at[chunk], OUT_A, OUT_A // 2)
        for chunk in range(NX)
    ]

    @pl.loop(0, NX)
    def _(at_x):
        neighbour_sum(at_x, (z + 4) % NZ, out_a)

    for chunk in range(NX):
        for way in (1, -1):
            reduces_a[chunk].send(0, way)

    @pl.loop(0, NX * (NZ - 1))
    def _(turn):
        neighbour_sum(turn % NX, (z + 5 + turn // NX) % NZ, out_a)

    def weight_products(kind):
        @pl.loop(0, 4)
        def _(tile):
            rows = pl.ds(pl.multiple_of(kind * WIDTH + tile * 256, 256), 256)
            product = dot(enc_sel[...], slots_t[rows, :], 1, 1).astype(BF16)
            w_part[kind, 2 * tile] = product[:, 0:TOK]
            w_part[kind, 2 * tile + 1] = product[:, TOK:]

    weight_products(1 - core)
    from_sibling = run.push(w_part.at[1 - core], w_pair, me.sibling())
    for chunk in range(NX):
        for way in (1, -1):
            reduces_a[chunk].send(1, way)
    weight_products(core)
    from_sibling.wait_recv()

    @pl.loop(0, NZ)
    def _(block):
        w_sum[block] = (w_part[core, block].astype(F32) + w_pair[block].astype(F32)).astype(BF16)

    reduce_w = Reduce(run, me, lambda block: w_sum.at[block], land_w, ENC, ENC // 2)
    reduce_b = Reduce(run, me, lambda block: b_sum.at[block], land_b, ENC - OUT_A, 96)

    def turn_of(reduces, hop):
        for reduce in reduces:
            for way in (1, -1):
                reduce.send(hop, way)

    turn_of([reduce_w], 0)
    turn_of([reduce_w], 1)
    turn_of(reduces_a, 2)
    turn_of([reduce_w], 2)
    turn_of([reduce_w], 3)
    for copy in from_x:
        copy.wait_recv()

    @pl.loop(0, NZ)
    def _(block):
        total = part[x, block, out_b].astype(F32)
        for step in range(NX - 1):
            total += x_b[step, block].astype(F32)
        b_sum[block] = total.astype(BF16)

    turn_of([reduce_b], 0)
    turn_of(reduces_a, 3)
    y_sum[pl.ds(0, ENC)] = reduce_w.end().astype(BF16)
    y_sum[pl.ds(ENC, 64)] = jnp.zeros((64, TOK), BF16)
    y = me.y
    from_y = []
    for step in range(1, NY):
        from_y.append(run.push(y_sum.at[rows_of((y + step) % NY)], y_land.at[step - 1], me.at_y(step)))
    turn_of([reduce_b], 1)
    total = y_sum[rows_of(y)].astype(F32)
    for step in range(1, NY):
        from_y[step - 1].wait_recv()
        total += y_land[step - 1].astype(F32)
    y_own[rows_of(y)] = total.astype(BF16)
    from_y = [run.push(y_own.at[rows_of(y)], y_own.at[rows_of(y)], me.at_y(step)) for step in range(1, NY)]
    turn_of([reduce_b], 2)
    from_x = {}
    for chunk in range(NX):
        a_sum[chunk] = reduces_a[chunk].end().astype(BF16)
    for step in (1, 3, 2):
        from_x[step] = run.push(a_sum.at[(x + step) % NX], x_a.at[step - 1], me.at_x(step))
    turn_of([reduce_b], 3)
    for copy in from_y:
        copy.wait_recv()
    w_own[...] = y_own[pl.ds(0, ENC)].astype(F32)
    from_sibling = run.push(w_own, w_other, me.sibling())
    total = a_sum[x].astype(F32)
    for step in (1, 3, 2):
        from_x[step].wait_recv()
        total += x_a[step - 1].astype(F32)
    out_enc[out_a] = total.astype(BF16)
    out_enc[out_b] = reduce_b.end().astype(BF16)
    from_sibling.wait_recv()

    @pl.when(core == 0)
    def _():
        out_w[0] = w_own[...]
        out_w[1] = w_other[...]

    @pl.when(core == 1)
    def _():
        out_w[0] = w_other[...]
        out_w[1] = w_own[...]

    for copy in late[7:]:
        copy.wait_recv()
    for copy in run.remote:
        copy.wait_send()
    run.local[-1].wait()


def rows_of(index):
    return pl.ds(pl.multiple_of(index * 64, 64), 64)


def whole(queries, out_grad, enc_t, key_weight, value_weight, ids):
    anywhere, vmem = pl.BlockSpec(memory_space=pl.ANY), pl.BlockSpec(memory_space=pltpu.VMEM)
    enc_b = ENC - OUT_A
    bf = lambda *shape: pltpu.VMEM(shape, BF16)
    f32 = lambda *shape: pltpu.VMEM(shape, F32)
    return pl.pallas_call(
        whole_kernel,
        out_shape=[
            jax.ShapeDtypeStruct((NX, TOK, WIDTH), BF16),
            jax.ShapeDtypeStruct((NX, 8, 128), jnp.int32),
            jax.ShapeDtypeStruct((ENC, NLEN), BF16),
            jax.ShapeDtypeStruct((2, ENC, TOK), F32),
        ],
        in_specs=[anywhere] * 6,
        out_specs=[anywhere, anywhere, vmem, vmem],
        scratch_shapes=[
            bf(NX, TOK, WIDTH),
            bf(NX, TOK, WIDTH),
            bf(NX, NZ, ENC, NLEN),
            bf(2, ENC, WIDTH),
            pltpu.SMEM((NX, 8, 128), jnp.int32),
            bf(ENC, SLOTS * NLEN),
            bf(2 * WIDTH, ENC),
            bf(2 * WIDTH, SLOTS * NLEN),
            bf(2 * WIDTH, SLOTS * NLEN),
            f32(HEADS_DEV * SPAN, 2 * NLEN),
            f32(HEADS_DEV * SPAN, 2 * NLEN),
            bf(HEADS_DEV * SPAN, 2 * NLEN),
            bf(HEADS_DEV * SPAN, 2 * NLEN),
            bf(NX, TOK, WIDTH),
            f32(SLOTS + 1, ENC, NLEN),
            bf(NX, NZ, ENC, NLEN),
            bf(2, NZ, ENC, TOK),
            bf(NZ, ENC, TOK),
            bf(NZ, ENC, TOK),
            bf(NX, 2, 4, OUT_A, NLEN),
            bf(2, 4, enc_b, NLEN),
            bf(2, 4, ENC, TOK),
            bf(NX - 1, NZ, enc_b, NLEN),
            bf(NZ, enc_b, NLEN),
            bf(NX, OUT_A, NLEN),
            bf(NX - 1, OUT_A, NLEN),
            bf(512, TOK),
            bf(NY - 1, 64, TOK),
            bf(512, TOK),
            f32(ENC, TOK),
            f32(ENC, TOK),
            pltpu.SemaphoreType.DMA((PUSHES,)),
            pltpu.SemaphoreType.DMA((PUSHES,)),
            pltpu.SemaphoreType.DMA((MOVES,)),
        ],
        compiler_params=pltpu.CompilerParams(collective_id=0, has_side_effects=True, vmem_limit_bytes=VMEM_LIMIT),
    )(queries, out_grad, enc_t, key_weight, value_weight, ids)


def close_kernel(q_ref, enc_ref, w_ref, out_q, out_enc, out_k, out_v, sems):
    copies = [
        pltpu.make_async_copy(q_ref.at[source], out_q.at[:, pl.ds(source * WIDTH, WIDTH)], sems.at[source])
        for source in range(NX)
    ]
    copies.append(pltpu.make_async_copy(enc_ref, out_enc, sems.at[4]))
    copies.append(pltpu.make_async_copy(w_ref.at[0], out_k, sems.at[5]))
    copies.append(pltpu.make_async_copy(w_ref.at[1], out_v, sems.at[6]))
    for copy in copies:
        copy.start()
    for copy in copies:
        copy.wait()


def close(query_grads, enc_grad, weight_grads):
    anywhere, vmem = pl.BlockSpec(memory_space=pl.ANY), pl.BlockSpec(memory_space=pltpu.VMEM)
    return pl.pallas_call(
        close_kernel,
        out_shape=[
            jax.ShapeDtypeStruct((TOK, NX * WIDTH), BF16),
            jax.ShapeDtypeStruct((ENC, NLEN), BF16),
            jax.ShapeDtypeStruct((ENC, TOK), F32),
            jax.ShapeDtypeStruct((ENC, TOK), F32),
        ],
        in_specs=[anywhere] * 3,
        out_specs=[vmem] * 4,
        scratch_shapes=[pltpu.SemaphoreType.DMA((7,))],
        compiler_params=pltpu.CompilerParams(vmem_limit_bytes=VMEM_LIMIT),
    )(query_grads, enc_grad, weight_grads)


def local(queries, out_grad, encodings, key_weight, value_weight, nbr_ids):
    enc_t = jnp.swapaxes(encodings[0], 0, 1)
    ids = jnp.pad(nbr_ids - lax.axis_index("dp") * (NX * NZ), ((0, 6), (0, 126)))
    query_grads, _, enc_grad, weight_grads = whole(queries, out_grad, enc_t, key_weight, value_weight, ids)
    query_grad, enc_grad, key_grad, value_grad = close(query_grads, enc_grad, weight_grads)
    return query_grad, jnp.swapaxes(enc_grad, 0, 1)[None], key_grad, value_grad


def solution(mesh):
    in_specs = (
        P(("dp", "group"), None),
        P(("dp", "group"), None),
        P(("dp", "group"), None, None),
        P(None, "group"),
        P(None, "group"),
        P(("dp", "group"), None),
    )
    out_specs = (
        P(("dp", "group"), None),
        P(("dp", "group"), None, None),
        P(None, "group"),
        P(None, "group"),
    )
    return jax.shard_map(local, mesh=mesh, in_specs=in_specs, out_specs=out_specs, check_vma=False)
```

time: 578 us -> 138 us (0.24)
  waiting for transfers between devices: 324 us -> 0 us
  Pallas kernels: 0 us -> 135 us
  matrix products: 95.6 us -> 0 us
  blocking collectives: 55.3 us -> 0 us
  other arithmetic: 42.7 us -> 0.01 us
  starting transfers between devices: 28.9 us -> 0 us
  between operations: 13.9 us -> 0.65 us
  local copies, waits for them, and re-layouts: 12.8 us -> 1.27 us
    reduce_scatter x1 -> x0, waiting for transfers between devices: 222 us -> none  [local(): lax.psum_scatter((term + jnp.einsum('ntf,ef->nte', value_grads, value_wei...]
    pallas_call x0 -> x2, Pallas kernels: none -> 135 us  [the longest x1 132 us: whole(): pl.pallas_call(whole_kernel, out_shape=[jax.ShapeDtypeStruct((NX, TOK, WI...]
    dot_general x11 -> x0, matrix products: 95.6 us -> none  [the longest x1 31.7 us: attend(): jnp.einsum('chqk,cqhd->ckhd', score_grads, query_four, preferred_element_...]
    psum x1 -> x0, waiting for transfers between devices: 70.1 us -> none  [local(): lax.psum(key_wgrad.astype(jnp.bfloat16), 'dp').astype(jnp.float32)]
    all_gather x1 -> x0, blocking collectives: 55.3 us -> none  [local(): slot_ids = lax.all_gather(nbr_ids, 'group', axis=0, tiled=True) - id_offset]
    scatter-add x2 -> x0, other arithmetic: 34.1 us -> none  [the longest x1 17 us: local(): jax.ops.segment_sum(key_slots, flat_ids, num_segments=group_neigh)]
    all_gather x1 -> x0, waiting for transfers between devices: 30.6 us -> none  [local(): enc_all = lax.all_gather(encodings, 'group', axis=0, tiled=True)]
    all_to_all x3 -> x0, starting transfers between devices: 28.6 us -> none  [the longest x1 13.7 us: local(): lax.all_to_all(out_grad, 'group', split_axis=1, concat_axis=0, tiled=True)]
  transfers between devices with their start and end apart: 6 -> 0, of which waited for: 3 -> 0; matrix products, arithmetic and copies ran while one was open for 11% -> 0% of each run, Pallas kernels for 0% -> 0%
where the time goes in v2:
time: 138 us; the launch traced here: 137 us
  Pallas kernels  135 us (98%)
    pallas_call x1, Pallas kernels, whole(): pl.pallas_call(whole_kernel, out_shape=[jax.ShapeDtypeStruct((NX, TOK, WI...  132 us

profile of v2, /device:TPU:1, one launch (start us, length us, event | category | flops | bytes accessed | tf_op | source)
XLA Modules:
  0.0 136.6 jit_solution(6068006209000221026)
XLA Ops:
  0.6 0.0 copy-start
  0.6 0.7 copy-done
  1.3 0.6 pad.4.ids_ref
  1.9 132.1 %shard_map.93 = (bf16[4,128,1024]{2,1,0:T(8,128)(2,1)}, s32[4,8,128]{2,1,0:T(8,128)}, bf16[448,128]{1,0:T(8,128)(2,1)}, f32[2,448,128]{2,1,0:T(8,128)}) custom-call(bf16[128,4096]{1,0:T(8,128)(2,1)} %q_ref.1, bf16[128,4096]{1,0:T(8,128)(2,1)} %g_ref.1, bf16[448,128]{1,0:T(8,128)(2,1)} %bitcast.6, bf16[448,128]{1,0:T(8,128)(2,1)} %kw_ref.1, ...), custom_call_target="tpu_custom_call" | custom-call | tf_op jit(solution)/shard_map/pallas_call | solution.py:418
  134.0 2.6 %shard_map.94 = (bf16[128,4096]{1,0:T(8,128)(2,1)}, bf16[448,128]{1,0:T(8,128)(2,1)}, f32[448,128]{1,0:T(8,128)}, f32[448,128]{1,0:T(8,128)}) custom-call(bf16[4,128,1024]{2,1,0:T(8,128)(2,1)} %get-tuple-element.11.q_ref, bf16[448,128]{1,0:T(8,128)(2,1)} %get-tuple-element.12.enc_ref, f32[2,448,128]{2,1,0:T(8,128)} %get-tuple-element.13.w_ref), custom_call_target="tpu_custom_call" | custom-call | tf_op jit(solution)/shard_map/pallas_call | solution.py:484
  (1 shorter events, 0.0 us)
Async XLA Ops:
  0.6 0.7 copy-start

commit v3 on v2

--- a/solution.py
+++ b/solution.py
@@ -16,8 +16,9 @@
 WIDTH = HEADS_DEV * HEAD_DIM
 SLOTS = 16
 TOK = 128
-IN_A = 336
-OUT_A = 256
+IN_A = 320
+OUT_A = 224
+QUARTER = ENC // 4
 MESH = pl.DeviceIdType.MESH
 BF16, F32 = jnp.bfloat16, jnp.float32
 VMEM_LIMIT = 60 * 1024 * 1024
@@ -35,8 +36,8 @@
     def at_z(self, step):
         return (self.dp, self.x * NZ + (self.z + step) % NZ)
 
-    def at_y(self, step):
-        return ((self.y + step) % NY * 2 + self.core, self.group)
+    def at_y(self, step, other=False):
+        return ((self.y + step) % NY * 2 + (1 - self.core if other else self.core), self.group)
 
     def sibling(self):
         return (self.y * 2 + 1 - self.core, self.group)
@@ -133,14 +134,14 @@
         return own + self.landed[0, 3].astype(F32) + self.landed[1, 3].astype(F32)
 
 
-PUSHES, MOVES = 160, 10
+PUSHES, MOVES = 168, 8
 
 
 def whole_kernel(
     q_ref, g_ref, enc_ref, kw_ref, vw_ref, ids_ref,
     out_q, ids_all, out_enc, out_w,
-    q_x, g_x, enc_all, w_all, ids, enc_sel, w_t, kv_t, slots_t, scores, grads, score_bf, weight_bf, qg,
-    slot_grads, part, w_part, w_pair, w_sum, land_a, land_b, land_w, x_b, b_sum, a_sum, x_a, y_sum, y_land, y_own, w_own, w_other,
+    q_x, g_x, enc_all, w_all, ids, table, enc_sel, w_t, kv_t, slots_t, scores, grads, score_bf, weight_bf, qg,
+    slot_grads, part_a, part_b, w_part, w_pair, w_sum, land_a, land_b, land_w, x_b, b_sum, a_sum, x_a, y_sum, y_land, y_all,
     send_sems, recv_sems, local_sems
 ):
     me = Place()
@@ -149,73 +150,115 @@
     meet(
         [me.at_x(1), me.at_x(2), me.at_x(3), me.at_z(1), me.at_z(NZ - 1), me.sibling()]
         + [me.at_y(step) for step in range(1, NY)]
+        + [me.at_y(step, other=True) for step in range(1, NY)]
     )
     run = Copies(send_sems, recv_sems, local_sems)
     late = []
 
     in_a, in_b = pl.ds(0, IN_A), pl.ds(IN_A, ENC - IN_A)
-    own_w = [run.move(kw_ref, w_all.at[0, :, cols(z, TOK)]), run.move(vw_ref, w_all.at[1, :, cols(z, TOK)])]
+    run.move(ids_ref, ids_all.at[x])
     own_enc = run.move(enc_ref, enc_all.at[x, z])
-    run.move(ids_ref, ids_all.at[x]).wait()
+    quarter = quarter_of(me.y)
+    own_w = [
+        pltpu.make_async_copy(ref.at[quarter], w_all.at[core, quarter, cols(z, TOK)], local_sems.at[MOVES])
+        for ref in (kw_ref, vw_ref)
+    ]
+    for kind in range(2):
+        pl.when(core == kind)(own_w[kind].start)
     gather_b = Gather(run, me, lambda block: enc_all.at[x, block, in_b], ENC - IN_A, 64)
-    for way in (1, -1):
-        gather_b.send(0, way, enc_ref.at[in_b])
+    gather_w = Gather(run, me, lambda block: w_all.at[core, quarter, cols(block, TOK)], QUARTER, 64)
+    gathers_a = [
+        Gather(run, me, lambda block, chunk=chunk: enc_all.at[(x + chunk) % NX, block, in_a], IN_A, 160)
+        for chunk in range(NX)
+    ]
+
+    def both_ways(gather, hop, source=None):
+        for way in (1, -1):
+            gather.send(hop, way, source)
+
+    both_ways(gather_b, 0, enc_ref.at[in_b])
     from_x = {}
     for step in (1, 3, 2):
         from_x[NX - step] = run.push(enc_ref.at[in_a], enc_all.at[x, z, in_a], me.at_x(step))
     lists = [run.push(ids_ref, ids_all.at[x], me.at_x(step)) for step in (1, 2, 3)]
-    for copy in own_w:
-        copy.wait()
-    gather_w = Gather(run, me, lambda block: w_all.at[core, :, cols(block, TOK)], ENC, ENC // 2)
-    for way in (1, -1):
-        gather_w.send(0, way)
+    own_w[0].wait()
+    both_ways(gather_w, 0)
+    both_ways(gathers_a[0], 0, enc_ref.at[in_a])
     inputs_x = {step: [] for step in range(NX)}
-    for step in (1, 3, 2):
-        for src, dst in ((q_ref, q_x), (g_ref, g_x)):
+
+    def exchange(src, dst):
+        for step in (1, 3, 2):
             copy = run.push(src.at[:, cols((x + step) % NX, WIDTH)], dst.at[x], me.at_x(step))
             inputs_x[NX - step].append(copy)
+
+    exchange(q_ref, q_x)
     own_inputs = [run.move(src.at[:, cols(x, WIDTH)], dst.at[x]) for src, dst in ((q_ref, q_x), (g_ref, g_x))]
-    gathers_a = {}
-    for chunk in (0, 1, 3, 2):
-        gathers_a[chunk] = Gather(
-            run, me, lambda block, chunk=chunk: enc_all.at[(x + chunk) % NX, block, in_a], IN_A, 176
-        )
     own_enc.wait()
-    for hop in range(4):
-        for way in (1, -1):
-            if hop > 0:
-                gather_b.send(hop, way)
-                block = gather_w.send(hop, way)
-                view = gather_w.view(block)
-                late.append(run.push(view, view, me.sibling()))
-        for chunk in (0, 1, 3, 2):
-            if hop == 0 and chunk != 0:
-                from_x[chunk].wait_recv()
-            for way in (1, -1):
-                gathers_a[chunk].send(hop, way)
+    both_ways(gather_b, 1)
+    both_ways(gather_w, 1)
+    for chunk in (1, 3):
+        from_x[chunk].wait_recv()
+        both_ways(gathers_a[chunk], 0)
+    both_ways(gather_b, 2)
+    both_ways(gather_w, 2)
+    from_x[2].wait_recv()
+    both_ways(gathers_a[2], 0)
+    both_ways(gather_b, 3)
+    both_ways(gather_w, 3)
+    both_ways(gathers_a[0], 1)
     gather_b.end()
     blocks_b = enc_all.at[x, :, in_b]
     from_x_b = [run.push(blocks_b, blocks_b, me.at_x(step)) for step in (1, 3, 2)]
+    exchange(g_ref, g_x)
     gather_w.end()
-    view = gather_w.view((z + 4) % NZ)
-    late.append(run.push(view, view, me.sibling()))
-    for copy in late:
+    own_quarter = w_all.at[core, quarter]
+    from_y = [run.push(own_quarter, own_quarter, me.at_y(step)) for step in (1, NY - 1, 2)]
+    from_sibling = [run.push(own_quarter, own_quarter, me.sibling())]
+    for chunk in (1, 3, 2):
+        both_ways(gathers_a[chunk], 1)
+    for chunk in (0, 1, 3, 2):
+        both_ways(gathers_a[chunk], 2)
+    for copy, step in zip(from_y, (3, 1, 2)):
+        copy.wait_recv()
+        view = w_all.at[core, quarter_of(me.y + step)]
+        from_sibling.append(run.push(view, view, me.sibling()))
+    for copy in lists:
+        copy.wait_recv()
+    run.local[0].wait()
+    run.move(ids_all, ids).wait()
+
+    def id_of(slot):
+        return ids[slot // 4, slot // 2 % 2, slot % 2] & (NX * NZ - 1)
+
+    def first_of(neighbour, after):
+        first = SLOTS
+        for slot in range(SLOTS - 1, after, -1):
+            first = jnp.where(id_of(slot) == neighbour, slot, first)
+        return first
+
+    def fill_table(start):
+        @pl.loop(start, start + NZ)
+        def _(neighbour):
+            table[neighbour] = first_of(neighbour, -1)
+
+    fill_table(0)
+    for turn, chunk in enumerate((0, 1, 3, 2)):
+        both_ways(gathers_a[chunk], 3)
+        if turn < 3:
+            fill_table((turn + 1) * NZ)
+    for slot in range(SLOTS):
+        table[NX * NZ + slot] = first_of(id_of(slot), slot)
+    for copy in from_sibling:
         copy.wait_recv()
     for kind in range(2):
         for head in range(HEADS_DEV):
             at = kind * WIDTH + head * HEAD_DIM
             w_t[at : at + HEAD_DIM, :] = w_all[kind, :, head * HEAD_DIM : (head + 1) * HEAD_DIM].T
-    slot_grads[SLOTS] = jnp.zeros((ENC, NLEN), F32)
-    for copy in lists:
-        copy.wait_recv()
-    run.move(ids_all, ids).wait()
+    slot_grads[SLOTS] = jnp.zeros((ENC, NLEN), BF16)
     for chunk in (0, 1, 3, 2):
         gathers_a[chunk].end()
     for copy in from_x_b:
         copy.wait_recv()
-
-    def id_of(slot):
-        return ids[slot // 4, slot // 2 % 2, slot % 2]
 
     for slot in range(SLOTS):
         neighbour = id_of(slot)
@@ -269,48 +312,63 @@
         def _(span):
             here = cols(span, 2 * NLEN)
             both = dot(w_all[0, rows, :], slots_t[0:WIDTH, here]) + dot(w_all[1, rows, :], slots_t[WIDTH:, here])
+            both = both.astype(BF16)
             slot_grads[2 * span, rows] = both[:, 0:NLEN]
             slot_grads[2 * span + 1, rows] = both[:, NLEN:]
 
-    def neighbour_sum(at_x, at_z, rows):
-        neighbour = at_x * NZ + at_z
-        total = None
-        for span in range(8):
-            first, second = id_of(2 * span), id_of(2 * span + 1)
-            slot = jnp.where(first == neighbour, 2 * span, jnp.where(second == neighbour, 2 * span + 1, SLOTS))
-            term = slot_grads[slot, rows]
-            total = term if total is None else total + term
-        part[at_x, at_z, rows] = total.astype(BF16)
+        for slot in range(SLOTS - 2, -1, -1):
+            slot_grads[slot, rows] = slot_grads[slot, rows] + slot_grads[table[NX * NZ + slot], rows]
+
+    def neighbour_a(at_x, at_z):
+        part_a[at_x, at_z] = slot_grads[table[at_x * NZ + at_z], out_a]
+
+    def sum_b(at_x):
+        @pl.loop(0, NZ)
+        def _(order):
+            part_b[at_x, order] = slot_grads[table[at_x * NZ + (z + 3 + order) % NZ], out_b]
 
     out_a, out_b = pl.ds(0, OUT_A), pl.ds(OUT_A, ENC - OUT_A)
-    slot_products(out_b)
-    from_x = []
-    for step in (1, 3, 2, 0):
-        at_x = (x + step) % NX
-
-        @pl.loop(0, NZ)
-        def _(at_z):
-            neighbour_sum(at_x, at_z, out_b)
-
-        if step != 0:
-            from_x.append(run.push(part.at[at_x, :, out_b], x_b.at[step - 1], me.at_x(step)))
-    slot_products(out_a)
     reduces_a = [
-        Reduce(run, me, lambda block, chunk=chunk: part.at[chunk, block, out_a], land_a.at[chunk], OUT_A, OUT_A // 2)
+        Reduce(run, me, lambda block, chunk=chunk: part_a.at[chunk, block], land_a.at[chunk], OUT_A, OUT_A // 2)
         for chunk in range(NX)
     ]
+    reduce_b = Reduce(
+        run, me, lambda block: b_sum.at[(block - z - 3 + 2 * NZ) % NZ], land_b, ENC - OUT_A, (ENC - OUT_A) // 2
+    )
+    reduce_w = Reduce(run, me, lambda block: w_sum.at[block], land_w, ENC, ENC // 2)
+
+    def turn_of(reduces, hop):
+        for reduce in reduces:
+            for way in (1, -1):
+                reduce.send(hop, way)
+
+    slot_products(out_a)
 
     @pl.loop(0, NX)
     def _(at_x):
-        neighbour_sum(at_x, (z + 4) % NZ, out_a)
-
-    for chunk in range(NX):
-        for way in (1, -1):
-            reduces_a[chunk].send(0, way)
+        neighbour_a(at_x, (z + 4) % NZ)
+
+    turn_of(reduces_a, 0)
+    slot_products(out_b)
+    half = (ENC - OUT_A) // 2
+    low, high = pl.ds(0, half), pl.ds(half, half)
+    far, right, left = (x + 2) % NX, (x + 1) % NX, (x + 3) % NX
+    groups = [pl.ds(0, 3), pl.ds(3, 5)]
+    sum_b(far)
+    sum_b(right)
+    sum_b(left)
+    via_left, via_right, high_left, low_right = [], [], [], []
+    for group in groups:
+        via_left.append(run.push(part_b.at[far, group, low], x_b.at[0, group], me.at_x(1)))
+        via_right.append(run.push(part_b.at[far, group, high], x_b.at[1, group], me.at_x(3)))
+        high_left.append(run.push(part_b.at[right, group, high], x_b.at[2, group], me.at_x(1)))
+        low_right.append(run.push(part_b.at[left, group, low], x_b.at[3, group], me.at_x(3)))
 
     @pl.loop(0, NX * (NZ - 1))
     def _(turn):
-        neighbour_sum(turn % NX, (z + 5 + turn // NX) % NZ, out_a)
+        neighbour_a(turn % NX, (z + 5 + turn // NX) % NZ)
+
+    turn_of(reduces_a, 1)
 
     def weight_products(kind):
         @pl.loop(0, 4)
@@ -322,88 +380,94 @@
 
     weight_products(1 - core)
     from_sibling = run.push(w_part.at[1 - core], w_pair, me.sibling())
-    for chunk in range(NX):
-        for way in (1, -1):
-            reduces_a[chunk].send(1, way)
+    sum_b(x)
     weight_products(core)
+
+    def add_on(target, landed, rows, group):
+        @pl.loop(*group)
+        def _(block):
+            landed[block] = (landed[block].astype(F32) + part_b[target, block, rows].astype(F32)).astype(BF16)
+
+    low_left, high_right = [], []
+
+    def pass_on(turn):
+        group, bounds = groups[turn], ((0, 3), (3, 8))[turn]
+        via_left[turn].wait_recv()
+        add_on(right, x_b.at[0], low, bounds)
+        low_left.append(run.push(x_b.at[0, group], x_b.at[4, group], me.at_x(1)))
+        via_right[turn].wait_recv()
+        add_on(left, x_b.at[1], high, bounds)
+        high_right.append(run.push(x_b.at[1, group], x_b.at[5, group], me.at_x(3)))
+
+    def end_x(turn):
+        for copies in (high_left, low_right, low_left, high_right):
+            copies[turn].wait_recv()
+
+        @pl.loop(*((0, 3), (3, 8))[turn])
+        def _(block):
+            for rows, first, second in ((low, 3, 4), (high, 2, 5)):
+                total = part_b[x, block, rows].astype(F32) + x_b[first, block].astype(F32)
+                b_sum[block, rows] = (total + x_b[second, block].astype(F32)).astype(BF16)
+
+    pass_on(0)
     from_sibling.wait_recv()
 
     @pl.loop(0, NZ)
     def _(block):
         w_sum[block] = (w_part[core, block].astype(F32) + w_pair[block].astype(F32)).astype(BF16)
 
-    reduce_w = Reduce(run, me, lambda block: w_sum.at[block], land_w, ENC, ENC // 2)
-    reduce_b = Reduce(run, me, lambda block: b_sum.at[block], land_b, ENC - OUT_A, 96)
-
-    def turn_of(reduces, hop):
-        for reduce in reduces:
-            for way in (1, -1):
-                reduce.send(hop, way)
-
     turn_of([reduce_w], 0)
+    turn_of(reduces_a, 2)
     turn_of([reduce_w], 1)
-    turn_of(reduces_a, 2)
+    pass_on(1)
+    turn_of(reduces_a[:2], 3)
     turn_of([reduce_w], 2)
+    turn_of(reduces_a[2:], 3)
+    end_x(0)
+    turn_of([reduce_b], 0)
     turn_of([reduce_w], 3)
-    for copy in from_x:
-        copy.wait_recv()
-
-    @pl.loop(0, NZ)
-    def _(block):
-        total = part[x, block, out_b].astype(F32)
-        for step in range(NX - 1):
-            total += x_b[step, block].astype(F32)
-        b_sum[block] = total.astype(BF16)
-
-    turn_of([reduce_b], 0)
-    turn_of(reduces_a, 3)
-    y_sum[pl.ds(0, ENC)] = reduce_w.end().astype(BF16)
-    y_sum[pl.ds(ENC, 64)] = jnp.zeros((64, TOK), BF16)
-    y = me.y
-    from_y = []
-    for step in range(1, NY):
-        from_y.append(run.push(y_sum.at[rows_of((y + step) % NY)], y_land.at[step - 1], me.at_y(step)))
     turn_of([reduce_b], 1)
-    total = y_sum[rows_of(y)].astype(F32)
-    for step in range(1, NY):
-        from_y[step - 1].wait_recv()
-        total += y_land[step - 1].astype(F32)
-    y_own[rows_of(y)] = total.astype(BF16)
-    from_y = [run.push(y_own.at[rows_of(y)], y_own.at[rows_of(y)], me.at_y(step)) for step in range(1, NY)]
-    turn_of([reduce_b], 2)
     from_x = {}
     for chunk in range(NX):
         a_sum[chunk] = reduces_a[chunk].end().astype(BF16)
     for step in (1, 3, 2):
         from_x[step] = run.push(a_sum.at[(x + step) % NX], x_a.at[step - 1], me.at_x(step))
+    y = me.y
+    y_sum[pl.ds(0, ENC)] = reduce_w.end().astype(BF16)
+    y_sum[pl.ds(ENC, 64)] = jnp.zeros((64, TOK), BF16)
+    from_y = []
+    for step in range(1, NY):
+        from_y.append(run.push(y_sum.at[rows_of((y + step) % NY)], y_land.at[step - 1], me.at_y(step)))
+    end_x(1)
+    turn_of([reduce_b], 2)
+    total = y_sum[rows_of(y)].astype(F32)
+    for step in range(1, NY):
+        from_y[step - 1].wait_recv()
+        total += y_land[step - 1].astype(F32)
+    y_all[core, rows_of(y)] = total.astype(BF16)
+    own_rows = y_all.at[core, rows_of(y)]
+    from_y = [run.push(own_rows, own_rows, me.at_y(step)) for step in range(1, NY)]
+    from_y += [run.push(own_rows, own_rows, me.at_y(step, other=True)) for step in range(NY)]
     turn_of([reduce_b], 3)
-    for copy in from_y:
-        copy.wait_recv()
-    w_own[...] = y_own[pl.ds(0, ENC)].astype(F32)
-    from_sibling = run.push(w_own, w_other, me.sibling())
     total = a_sum[x].astype(F32)
     for step in (1, 3, 2):
         from_x[step].wait_recv()
         total += x_a[step - 1].astype(F32)
     out_enc[out_a] = total.astype(BF16)
+    for copy in from_y:
+        copy.wait_recv()
+    for kind in range(2):
+        out_w[kind] = y_all[kind, pl.ds(0, ENC)].astype(F32)
     out_enc[out_b] = reduce_b.end().astype(BF16)
-    from_sibling.wait_recv()
-
-    @pl.when(core == 0)
-    def _():
-        out_w[0] = w_own[...]
-        out_w[1] = w_other[...]
-
-    @pl.when(core == 1)
-    def _():
-        out_w[0] = w_other[...]
-        out_w[1] = w_own[...]
-
-    for copy in late[7:]:
+    for copy in late:
         copy.wait_recv()
     for copy in run.remote:
         copy.wait_send()
     run.local[-1].wait()
+
+
+def quarter_of(index):
+    return pl.ds(pl.multiple_of(index % 4 * QUARTER, QUARTER), QUARTER)
 
 
 def rows_of(index):
@@ -419,7 +483,7 @@
         whole_kernel,
         out_shape=[
             jax.ShapeDtypeStruct((NX, TOK, WIDTH), BF16),
-            jax.ShapeDtypeStruct((NX, 8, 128), jnp.int32),
+            jax.ShapeDtypeStruct((NX, 2, 2), jnp.int32),
             jax.ShapeDtypeStruct((ENC, NLEN), BF16),
             jax.ShapeDtypeStruct((2, ENC, TOK), F32),
         ],
@@ -430,7 +494,8 @@
             bf(NX, TOK, WIDTH),
             bf(NX, NZ, ENC, NLEN),
             bf(2, ENC, WIDTH),
-            pltpu.SMEM((NX, 8, 128), jnp.int32),
+            pltpu.SMEM((NX, 2, 2), jnp.int32),
+            pltpu.SMEM((NX * NZ + SLOTS,), jnp.int32),
             bf(ENC, SLOTS * NLEN),
             bf(2 * WIDTH, ENC),
             bf(2 * WIDTH, SLOTS * NLEN),
@@ -440,26 +505,25 @@
             bf(HEADS_DEV * SPAN, 2 * NLEN),
             bf(HEADS_DEV * SPAN, 2 * NLEN),
             bf(NX, TOK, WIDTH),
-            f32(SLOTS + 1, ENC, NLEN),
-            bf(NX, NZ, ENC, NLEN),
+            bf(SLOTS + 1, ENC, NLEN),
+            bf(NX, NZ, OUT_A, NLEN),
+            bf(NX, NZ, enc_b, NLEN),
             bf(2, NZ, ENC, TOK),
             bf(NZ, ENC, TOK),
             bf(NZ, ENC, TOK),
             bf(NX, 2, 4, OUT_A, NLEN),
             bf(2, 4, enc_b, NLEN),
             bf(2, 4, ENC, TOK),
-            bf(NX - 1, NZ, enc_b, NLEN),
+            bf(6, NZ, enc_b // 2, NLEN),
             bf(NZ, enc_b, NLEN),
             bf(NX, OUT_A, NLEN),
             bf(NX - 1, OUT_A, NLEN),
             bf(512, TOK),
             bf(NY - 1, 64, TOK),
-            bf(512, TOK),
-            f32(ENC, TOK),
-            f32(ENC, TOK),
+            bf(2, 512, TOK),
             pltpu.SemaphoreType.DMA((PUSHES,)),
             pltpu.SemaphoreType.DMA((PUSHES,)),
-            pltpu.SemaphoreType.DMA((MOVES,)),
+            pltpu.SemaphoreType.DMA((MOVES + 1,)),
         ],
         compiler_params=pltpu.CompilerParams(collective_id=0, has_side_effects=True, vmem_limit_bytes=VMEM_LIMIT),
     )(queries, out_grad, enc_t, key_weight, value_weight, ids)
@@ -498,8 +562,7 @@
 
 def local(queries, out_grad, encodings, key_weight, value_weight, nbr_ids):
     enc_t = jnp.swapaxes(encodings[0], 0, 1)
-    ids = jnp.pad(nbr_ids - lax.axis_index("dp") * (NX * NZ), ((0, 6), (0, 126)))
-    query_grads, _, enc_grad, weight_grads = whole(queries, out_grad, enc_t, key_weight, value_weight, ids)
+    query_grads, _, enc_grad, weight_grads = whole(queries, out_grad, enc_t, key_weight, value_weight, nbr_ids)
     query_grad, enc_grad, key_grad, value_grad = close(query_grads, enc_grad, weight_grads)
     return query_grad, jnp.swapaxes(enc_grad, 0, 1)[None], key_grad, value_grad
 

time: 138 us -> 124 us (0.90); the launches traced: 137 us -> 124 us
  Pallas kernels: 135 us -> 123 us
    pallas_call x1, Pallas kernels: 132 us -> 121 us  [whole(): pl.pallas_call(whole_kernel, out_shape=[jax.ShapeDtypeStruct((NX, TOK, WI...]
where the time goes in v3:
time: 124 us
  Pallas kernels  123 us (99%)
    pallas_call x1, Pallas kernels, whole(): pl.pallas_call(whole_kernel, out_shape=[jax.ShapeDtypeStruct((NX, TOK, WI...  121 us
    pallas_call x1, Pallas kernels, close(): pl.pallas_call(close_kernel, out_shape=[jax.ShapeDtypeStruct((TOK, NX * W...  2.57 us

profile of v3, /device:TPU:1, one launch (start us, length us, event | category | flops | bytes accessed | tf_op | source)
XLA Modules:
  0.0 124.1 jit_solution(3059322399774021573)
XLA Ops:
  0.6 120.9 %shard_map.93 = (bf16[4,128,1024]{2,1,0:T(8,128)(2,1)}, s32[4,2,2]{2,1,0:T(2,128)}, bf16[448,128]{1,0:T(8,128)(2,1)}, f32[2,448,128]{2,1,0:T(8,128)}) custom-call(bf16[128,4096]{1,0:T(8,128)(2,1)} %q_ref.1, bf16[128,4096]{1,0:T(8,128)(2,1)} %g_ref.1, bf16[448,128]{1,0:T(8,128)(2,1)} %bitcast.6, bf16[448,128]{1,0:T(8,128)(2,1)} %kw_ref.1, ...), custom_call_target="tpu_custom_call" | custom-call | tf_op jit(solution)/shard_map/pallas_call | solution.py:482
  121.5 2.6 %shard_map.94 = (bf16[128,4096]{1,0:T(8,128)(2,1)}, bf16[448,128]{1,0:T(8,128)(2,1)}, f32[448,128]{1,0:T(8,128)}, f32[448,128]{1,0:T(8,128)}) custom-call(bf16[4,128,1024]{2,1,0:T(8,128)(2,1)} %get-tuple-element.11.q_ref, bf16[448,128]{1,0:T(8,128)(2,1)} %get-tuple-element.12.enc_ref, f32[2,448,128]{2,1,0:T(8,128)} %get-tuple-element.13.w_ref), custom_call_target="tpu_custom_call" | custom-call | tf_op jit(solution)/shard_map/pallas_call | solution.py:548

commit v4 on v3

--- a/solution.py
+++ b/solution.py
@@ -17,7 +17,7 @@
 SLOTS = 16
 TOK = 128
 IN_A = 320
-OUT_A = 224
+OUT_A = 160
 QUARTER = ENC // 4
 MESH = pl.DeviceIdType.MESH
 BF16, F32 = jnp.bfloat16, jnp.float32
@@ -135,6 +135,14 @@
 
 
 PUSHES, MOVES = 168, 8
+ORDER = (
+    "w_other", "w_own", "w_pair_up", "w0", "b_products", "b_over_x",
+    "w1", "a_products", "a_first", "a0", "a_rest", "w2",
+    "b_own", "b_pass_on_0", "a1", "w3", "b_pass_on_1", "a2",
+    "w_over_y", "b_sum_up_0", "b0", "a3", "w_hand_on", "b1",
+    "a_over_x", "b_sum_up_1", "b2", "a_end", "w_end", "b3",
+    "b_end",
+)
 
 
 def whole_kernel(
@@ -328,47 +336,83 @@
             part_b[at_x, order] = slot_grads[table[at_x * NZ + (z + 3 + order) % NZ], out_b]
 
     out_a, out_b = pl.ds(0, OUT_A), pl.ds(OUT_A, ENC - OUT_A)
+    half = (ENC - OUT_A) // 2
+    low, high = pl.ds(0, half), pl.ds(half, half)
+    far, right, left = (x + 2) % NX, (x + 1) % NX, (x + 3) % NX
+    groups, bounds = [pl.ds(0, 3), pl.ds(3, 5)], [(0, 3), (3, 8)]
+    y = me.y
+    going = {}
     reduces_a = [
         Reduce(run, me, lambda block, chunk=chunk: part_a.at[chunk, block], land_a.at[chunk], OUT_A, OUT_A // 2)
         for chunk in range(NX)
     ]
-    reduce_b = Reduce(
-        run, me, lambda block: b_sum.at[(block - z - 3 + 2 * NZ) % NZ], land_b, ENC - OUT_A, (ENC - OUT_A) // 2
-    )
+    reduce_b = Reduce(run, me, lambda block: b_sum.at[(block - z - 3 + 2 * NZ) % NZ], land_b, ENC - OUT_A, half)
     reduce_w = Reduce(run, me, lambda block: w_sum.at[block], land_w, ENC, ENC // 2)
 
-    def turn_of(reduces, hop):
+    def turn(reduces, hop):
         for reduce in reduces:
             for way in (1, -1):
                 reduce.send(hop, way)
 
-    slot_products(out_a)
-
-    @pl.loop(0, NX)
-    def _(at_x):
-        neighbour_a(at_x, (z + 4) % NZ)
-
-    turn_of(reduces_a, 0)
-    slot_products(out_b)
-    half = (ENC - OUT_A) // 2
-    low, high = pl.ds(0, half), pl.ds(half, half)
-    far, right, left = (x + 2) % NX, (x + 1) % NX, (x + 3) % NX
-    groups = [pl.ds(0, 3), pl.ds(3, 5)]
-    sum_b(far)
-    sum_b(right)
-    sum_b(left)
-    via_left, via_right, high_left, low_right = [], [], [], []
-    for group in groups:
-        via_left.append(run.push(part_b.at[far, group, low], x_b.at[0, group], me.at_x(1)))
-        via_right.append(run.push(part_b.at[far, group, high], x_b.at[1, group], me.at_x(3)))
-        high_left.append(run.push(part_b.at[right, group, high], x_b.at[2, group], me.at_x(1)))
-        low_right.append(run.push(part_b.at[left, group, low], x_b.at[3, group], me.at_x(3)))
-
-    @pl.loop(0, NX * (NZ - 1))
-    def _(turn):
-        neighbour_a(turn % NX, (z + 5 + turn // NX) % NZ)
-
-    turn_of(reduces_a, 1)
+    def a_first():
+        @pl.loop(0, NX)
+        def _(at_x):
+            neighbour_a(at_x, (z + 4) % NZ)
+
+    def a_rest():
+        @pl.loop(0, NX * (NZ - 1))
+        def _(index):
+            neighbour_a(index % NX, (z + 5 + index // NX) % NZ)
+
+    def a_over_x():
+        for chunk in range(NX):
+            a_sum[chunk] = reduces_a[chunk].end().astype(BF16)
+        going["a"] = [run.push(a_sum.at[(x + step) % NX], x_a.at[step - 1], me.at_x(step)) for step in (1, 2, 3)]
+
+    def a_end():
+        total = a_sum[x].astype(F32)
+        for step in range(NX - 1):
+            going["a"][step].wait_recv()
+            total += x_a[step].astype(F32)
+        out_enc[out_a] = total.astype(BF16)
+
+    def b_over_x():
+        for at_x in (far, right, left):
+            sum_b(at_x)
+        going["b"] = []
+        for group in groups:
+            via_left = run.push(part_b.at[far, group, low], x_b.at[0, group], me.at_x(1))
+            via_right = run.push(part_b.at[far, group, high], x_b.at[1, group], me.at_x(3))
+            high_left = run.push(part_b.at[right, group, high], x_b.at[2, group], me.at_x(1))
+            low_right = run.push(part_b.at[left, group, low], x_b.at[3, group], me.at_x(3))
+            going["b"].append([via_left, via_right, high_left, low_right])
+
+    def add_on(target, landed, rows, blocks):
+        @pl.loop(*blocks)
+        def _(block):
+            landed[block] = (landed[block].astype(F32) + part_b[target, block, rows].astype(F32)).astype(BF16)
+
+    def b_pass_on(at):
+        group, copies = groups[at], going["b"][at]
+        copies[0].wait_recv()
+        add_on(right, x_b.at[0], low, bounds[at])
+        copies[0] = run.push(x_b.at[0, group], x_b.at[4, group], me.at_x(1))
+        copies[1].wait_recv()
+        add_on(left, x_b.at[1], high, bounds[at])
+        copies[1] = run.push(x_b.at[1, group], x_b.at[5, group], me.at_x(3))
+
+    def b_sum_up(at):
+        for copy in going["b"][at]:
+            copy.wait_recv()
+
+        @pl.loop(*bounds[at])
+        def _(block):
+            for rows, first, second in ((low, 3, 4), (high, 2, 5)):
+                total = part_b[x, block, rows].astype(F32) + x_b[first, block].astype(F32)
+                b_sum[block, rows] = (total + x_b[second, block].astype(F32)).astype(BF16)
+
+    def b_end():
+        out_enc[out_b] = reduce_b.end().astype(BF16)
 
     def weight_products(kind):
         @pl.loop(0, 4)
@@ -378,87 +422,76 @@
             w_part[kind, 2 * tile] = product[:, 0:TOK]
             w_part[kind, 2 * tile + 1] = product[:, TOK:]
 
-    weight_products(1 - core)
-    from_sibling = run.push(w_part.at[1 - core], w_pair, me.sibling())
-    sum_b(x)
-    weight_products(core)
-
-    def add_on(target, landed, rows, group):
-        @pl.loop(*group)
+    def w_other():
+        weight_products(1 - core)
+        going["pair"] = run.push(w_part.at[1 - core], w_pair, me.sibling())
+
+    def w_pair_up():
+        going["pair"].wait_recv()
+
+        @pl.loop(0, NZ)
         def _(block):
-            landed[block] = (landed[block].astype(F32) + part_b[target, block, rows].astype(F32)).astype(BF16)
-
-    low_left, high_right = [], []
-
-    def pass_on(turn):
-        group, bounds = groups[turn], ((0, 3), (3, 8))[turn]
-        via_left[turn].wait_recv()
-        add_on(right, x_b.at[0], low, bounds)
-        low_left.append(run.push(x_b.at[0, group], x_b.at[4, group], me.at_x(1)))
-        via_right[turn].wait_recv()
-        add_on(left, x_b.at[1], high, bounds)
-        high_right.append(run.push(x_b.at[1, group], x_b.at[5, group], me.at_x(3)))
-
-    def end_x(turn):
-        for copies in (high_left, low_right, low_left, high_right):
-            copies[turn].wait_recv()
-
-        @pl.loop(*((0, 3), (3, 8))[turn])
-        def _(block):
-            for rows, first, second in ((low, 3, 4), (high, 2, 5)):
-                total = part_b[x, block, rows].astype(F32) + x_b[first, block].astype(F32)
-                b_sum[block, rows] = (total + x_b[second, block].astype(F32)).astype(BF16)
-
-    pass_on(0)
-    from_sibling.wait_recv()
-
-    @pl.loop(0, NZ)
-    def _(block):
-        w_sum[block] = (w_part[core, block].astype(F32) + w_pair[block].astype(F32)).astype(BF16)
-
-    turn_of([reduce_w], 0)
-    turn_of(reduces_a, 2)
-    turn_of([reduce_w], 1)
-    pass_on(1)
-    turn_of(reduces_a[:2], 3)
-    turn_of([reduce_w], 2)
-    turn_of(reduces_a[2:], 3)
-    end_x(0)
-    turn_of([reduce_b], 0)
-    turn_of([reduce_w], 3)
-    turn_of([reduce_b], 1)
-    from_x = {}
-    for chunk in range(NX):
-        a_sum[chunk] = reduces_a[chunk].end().astype(BF16)
-    for step in (1, 3, 2):
-        from_x[step] = run.push(a_sum.at[(x + step) % NX], x_a.at[step - 1], me.at_x(step))
-    y = me.y
-    y_sum[pl.ds(0, ENC)] = reduce_w.end().astype(BF16)
-    y_sum[pl.ds(ENC, 64)] = jnp.zeros((64, TOK), BF16)
-    from_y = []
-    for step in range(1, NY):
-        from_y.append(run.push(y_sum.at[rows_of((y + step) % NY)], y_land.at[step - 1], me.at_y(step)))
-    end_x(1)
-    turn_of([reduce_b], 2)
-    total = y_sum[rows_of(y)].astype(F32)
-    for step in range(1, NY):
-        from_y[step - 1].wait_recv()
-        total += y_land[step - 1].astype(F32)
-    y_all[core, rows_of(y)] = total.astype(BF16)
-    own_rows = y_all.at[core, rows_of(y)]
-    from_y = [run.push(own_rows, own_rows, me.at_y(step)) for step in range(1, NY)]
-    from_y += [run.push(own_rows, own_rows, me.at_y(step, other=True)) for step in range(NY)]
-    turn_of([reduce_b], 3)
-    total = a_sum[x].astype(F32)
-    for step in (1, 3, 2):
-        from_x[step].wait_recv()
-        total += x_a[step - 1].astype(F32)
-    out_enc[out_a] = total.astype(BF16)
-    for copy in from_y:
-        copy.wait_recv()
-    for kind in range(2):
-        out_w[kind] = y_all[kind, pl.ds(0, ENC)].astype(F32)
-    out_enc[out_b] = reduce_b.end().astype(BF16)
+            w_sum[block] = (w_part[core, block].astype(F32) + w_pair[block].astype(F32)).astype(BF16)
+
+    def w_over_y():
+        y_sum[pl.ds(0, ENC)] = reduce_w.end().astype(BF16)
+        y_sum[pl.ds(ENC, 64)] = jnp.zeros((64, TOK), BF16)
+        going["y"] = [
+            run.push(y_sum.at[rows_of((y + step) % NY)], y_land.at[step - 1], me.at_y(step)) for step in range(1, NY)
+        ]
+
+    def w_hand_on():
+        total = y_sum[rows_of(y)].astype(F32)
+        for step in range(NY - 1):
+            going["y"][step].wait_recv()
+            total += y_land[step].astype(F32)
+        y_all[core, rows_of(y)] = total.astype(BF16)
+        own_rows = y_all.at[core, rows_of(y)]
+        going["y"] = [run.push(own_rows, own_rows, me.at_y(step)) for step in range(1, NY)]
+        going["y"] += [run.push(own_rows, own_rows, me.at_y(step, other=True)) for step in range(NY)]
+
+    def w_end():
+        for copy in going["y"]:
+            copy.wait_recv()
+        for kind in range(2):
+            out_w[kind] = y_all[kind, pl.ds(0, ENC)].astype(F32)
+
+    steps = {
+        "a_products": lambda: slot_products(out_a),
+        "a_first": a_first,
+        "a_rest": a_rest,
+        "a0": lambda: turn(reduces_a, 0),
+        "a1": lambda: turn(reduces_a, 1),
+        "a2": lambda: turn(reduces_a, 2),
+        "a3": lambda: turn(reduces_a, 3),
+        "a_over_x": a_over_x,
+        "a_end": a_end,
+        "b_products": lambda: slot_products(out_b),
+        "b_over_x": b_over_x,
+        "b_own": lambda: sum_b(x),
+        "b_pass_on_0": lambda: b_pass_on(0),
+        "b_pass_on_1": lambda: b_pass_on(1),
+        "b_sum_up_0": lambda: b_sum_up(0),
+        "b_sum_up_1": lambda: b_sum_up(1),
+        "b0": lambda: turn([reduce_b], 0),
+        "b1": lambda: turn([reduce_b], 1),
+        "b2": lambda: turn([reduce_b], 2),
+        "b3": lambda: turn([reduce_b], 3),
+        "b_end": b_end,
+        "w_other": w_other,
+        "w_own": lambda: weight_products(core),
+        "w_pair_up": w_pair_up,
+        "w0": lambda: turn([reduce_w], 0),
+        "w1": lambda: turn([reduce_w], 1),
+        "w2": lambda: turn([reduce_w], 2),
+        "w3": lambda: turn([reduce_w], 3),
+        "w_over_y": w_over_y,
+        "w_hand_on": w_hand_on,
+        "w_end": w_end,
+    }
+    for name in ORDER:
+        steps[name]()
+
     for copy in late:
         copy.wait_recv()
     for copy in run.remote:

time: 124 us -> 118 us (0.952)
  Pallas kernels: 123 us -> 118 us
    pallas_call x1, Pallas kernels: 121 us -> 115 us  [whole(): pl.pallas_call(whole_kernel, out_shape=[jax.ShapeDtypeStruct((NX, TOK, WI...]
where the time goes in v4:
time: 118 us
  Pallas kernels  118 us (100%)
    pallas_call x1, Pallas kernels, whole(): pl.pallas_call(whole_kernel, out_shape=[jax.ShapeDtypeStruct((NX, TOK, WI...  115 us
    pallas_call x1, Pallas kernels, close(): pl.pallas_call(close_kernel, out_shape=[jax.ShapeDtypeStruct((TOK, NX * W...  2.57 us

profile of v4, /device:TPU:1, one launch (start us, length us, event | category | flops | bytes accessed | tf_op | source)
XLA Modules:
  0.0 118.3 jit_solution(482495486697260430)
XLA Ops:
  0.6 115.1 %shard_map.93 = (bf16[4,128,1024]{2,1,0:T(8,128)(2,1)}, s32[4,2,2]{2,1,0:T(2,128)}, bf16[448,128]{1,0:T(8,128)(2,1)}, f32[2,448,128]{2,1,0:T(8,128)}) custom-call(bf16[128,4096]{1,0:T(8,128)(2,1)} %q_ref.1, bf16[128,4096]{1,0:T(8,128)(2,1)} %g_ref.1, bf16[448,128]{1,0:T(8,128)(2,1)} %bitcast.6, bf16[448,128]{1,0:T(8,128)(2,1)} %kw_ref.1, ...), custom_call_target="tpu_custom_call" | custom-call | tf_op jit(solution)/shard_map/pallas_call | solution.py:515
  115.7 2.6 %shard_map.94 = (bf16[128,4096]{1,0:T(8,128)(2,1)}, bf16[448,128]{1,0:T(8,128)(2,1)}, f32[448,128]{1,0:T(8,128)}, f32[448,128]{1,0:T(8,128)}) custom-call(bf16[4,128,1024]{2,1,0:T(8,128)(2,1)} %get-tuple-element.11.q_ref, bf16[448,128]{1,0:T(8,128)(2,1)} %get-tuple-element.12.enc_ref, f32[2,448,128]{2,1,0:T(8,128)} %get-tuple-element.13.w_ref), custom_call_target="tpu_custom_call" | custom-call | tf_op jit(solution)/shard_map/pallas_call | solution.py:581

commit v5 on v4

--- a/solution.py
+++ b/solution.py
@@ -16,7 +16,7 @@
 WIDTH = HEADS_DEV * HEAD_DIM
 SLOTS = 16
 TOK = 128
-IN_A = 320
+IN_A = 288
 OUT_A = 160
 QUARTER = ENC // 4
 MESH = pl.DeviceIdType.MESH
@@ -280,7 +280,7 @@
             rows = pl.ds(tile * 512, 512)
             kv_t[rows, here] = dot(w_t[rows, :], chosen).astype(BF16)
 
-    for step in (1, 3, 2, 0):
+    for step in (0, 1, 3, 2):
         source = (x + step) % NX
         if step == 0:
             for copy in own_inputs:

time: 118 us -> 118 us (level)
  no operation moved by 1% of the time
where the time goes in v5:
time: 118 us; the launch traced here: 117 us
  Pallas kernels  117 us (99%)
    pallas_call x1, Pallas kernels, whole(): pl.pallas_call(whole_kernel, out_shape=[jax.ShapeDtypeStruct((NX, TOK, WI...  114 us
    pallas_call x1, Pallas kernels, close(): pl.pallas_call(close_kernel, out_shape=[jax.ShapeDtypeStruct((TOK, NX * W...  2.57 us

profile of v5, /device:TPU:1, one launch (start us, length us, event | category | flops | bytes accessed | tf_op | source)
XLA Modules:
  0.0 117.2 jit_solution(5340629434508765190)
XLA Ops:
  0.6 114.0 %shard_map.93 = (bf16[4,128,1024]{2,1,0:T(8,128)(2,1)}, s32[4,2,2]{2,1,0:T(2,128)}, bf16[448,128]{1,0:T(8,128)(2,1)}, f32[2,448,128]{2,1,0:T(8,128)}) custom-call(bf16[128,4096]{1,0:T(8,128)(2,1)} %q_ref.1, bf16[128,4096]{1,0:T(8,128)(2,1)} %g_ref.1, bf16[448,128]{1,0:T(8,128)(2,1)} %bitcast.6, bf16[448,128]{1,0:T(8,128)(2,1)} %kw_ref.1, ...), custom_call_target="tpu_custom_call" | custom-call | tf_op jit(solution)/shard_map/pallas_call | solution.py:515
  114.6 2.6 %shard_map.94 = (bf16[128,4096]{1,0:T(8,128)(2,1)}, bf16[448,128]{1,0:T(8,128)(2,1)}, f32[448,128]{1,0:T(8,128)}, f32[448,128]{1,0:T(8,128)}) custom-call(bf16[4,128,1024]{2,1,0:T(8,128)(2,1)} %get-tuple-element.11.q_ref, bf16[448,128]{1,0:T(8,128)(2,1)} %get-tuple-element.12.enc_ref, f32[2,448,128]{2,1,0:T(8,128)} %get-tuple-element.13.w_ref), custom_call_target="tpu_custom_call" | custom-call | tf_op jit(solution)/shard_map/pallas_call | solution.py:581
